TPU v7x, 32 devices: a whole 2x2x4 slice. The times are simulated.
32 devices in a mesh: dp: 16 (over z, y, core), tensor: 2 (over x).
Axes of the slice: x: 2, y: 2, z: 4, core: 2. Of those that a mesh axis runs over, the one named last changes fastest.
Arguments:
- latent_tokens: bfloat16 [512, 32, 1152], P('tensor', 'dp'), may hold values from -6 to 6
- cond: bfloat16 [32, 1152], P('dp'), may hold values from -6 to 6
- mod_weight: bfloat16 [1152, 6, 1152], P('dp', None, 'tensor'), may hold values from -0.1875 to 0.1875
- qkv_weight: bfloat16 [1152, 3, 1152], P('dp', None, 'tensor'), may hold values from -0.1875 to 0.1875
- out_weight: bfloat16 [1152, 1152], P('tensor', 'dp'), may hold values from -0.75 to 0.75
- fc1_weight: bfloat16 [1152, 4608], P('dp', 'tensor'), may hold values from -0.1875 to 0.1875
- fc2_weight: bfloat16 [4608, 1152], P('tensor', 'dp'), may hold values from -0.09375 to 0.09375
- grad_out: bfloat16 [512, 32, 1152], P('tensor', 'dp'), may hold values from -6 to 6
Outputs:
- block_output: bfloat16 [512, 32, 1152], P('tensor', 'dp')
- grad_x: float32 [512, 32, 1152], P('tensor', 'dp')
- grad_cond: float32 [32, 1152], P('dp')
- grad_mod_weight: float32 [1152, 6, 1152], P('dp', None, 'tensor')
- grad_qkv_weight: float32 [1152, 3, 1152], P('dp', None, 'tensor')
- grad_out_weight: float32 [1152, 1152], P('tensor', 'dp')
- grad_fc1_weight: float32 [1152, 4608], P('dp', 'tensor')
- grad_fc2_weight: float32 [4608, 1152], P('tensor', 'dp')
All inputs are finite; a program needn't handle non-finite values.
Results may differ from a plain program's by a relative error of at most 0.022.
The roundings to bfloat16 on the way count: a program that leaves them out, or rounds other values in their place, can miss the bound.
Values may be sent and summed in bfloat16 or wider, within the bound.
A program may use at most 192 MiB of HBM per device.

v0:
```python
import jax
import jax.numpy as jnp
from jax import lax
from jax.sharding import PartitionSpec as P

HEAD_DIM = 72


eps_norm = 1e-06


def layer_norm(values):
    centred = values - jnp.mean(values, axis=-1, keepdims=True)
    recip = lax.rsqrt(jnp.mean(centred * centred, axis=-1, keepdims=True) + eps_norm)
    return (centred * recip, recip)


def norm_back(grad_norm, normed, recip):
    inner = grad_norm - jnp.mean(grad_norm, axis=-1, keepdims=True)
    return recip * (inner - normed * jnp.mean(grad_norm * normed, axis=-1, keepdims=True))


def attend_one(queries, key_rows, value_rows):
    scores = jnp.einsum(
        "qhe,khe->hqk", queries, key_rows, preferred_element_type=jnp.float32
    ) * HEAD_DIM ** (-0.5)
    peak = jnp.max(scores, axis=-1, keepdims=True)
    raised = jnp.exp(scores - peak)
    total = jnp.sum(raised, axis=-1, keepdims=True)
    attn_probs = (raised / total).astype(jnp.bfloat16)
    attended = jnp.einsum(
        "hqk,khe->qhe", attn_probs, value_rows, preferred_element_type=jnp.float32
    )
    return (attended.astype(jnp.bfloat16), peak + jnp.log(total))


def attend_back(queries, key_rows, value_rows, grad_att, log_total):
    scale = HEAD_DIM ** (-0.5)
    scores = (
        jnp.einsum("qhe,khe->hqk", queries, key_rows, preferred_element_type=jnp.float32) * scale
    )
    attn_probs = jnp.exp(scores - log_total)
    probs_low = attn_probs.astype(jnp.bfloat16)
    grad_probs = jnp.einsum(
        "qhe,khe->hqk", grad_att, value_rows, preferred_element_type=jnp.float32
    )
    centre = jnp.sum(attn_probs * grad_probs, axis=-1, keepdims=True)
    grad_scores = (attn_probs * (grad_probs - centre)).astype(jnp.bfloat16)
    grad_q = (
        jnp.einsum("hqk,khe->qhe", grad_scores, key_rows, preferred_element_type=jnp.float32)
        * scale
    )
    grad_k = (
        jnp.einsum("hqk,qhe->khe", grad_scores, queries, preferred_element_type=jnp.float32) * scale
    )
    grad_v = jnp.einsum("hqk,qhe->khe", probs_low, grad_att, preferred_element_type=jnp.float32)
    return jnp.stack([grad_q, grad_k, grad_v], axis=1).astype(jnp.bfloat16)


def body(latent_tokens, cond, mod_weight, qkv_weight, out_weight, fc1_weight, fc2_weight, grad_out):
    (
        modulation_weight,
        query_key_value_weight,
        output_projection_weight,
        first_dense_weight,
        second_dense_weight,
    ) = (
        lax.all_gather(mod_weight, "dp", axis=0, tiled=True),
        lax.all_gather(qkv_weight, "dp", axis=0, tiled=True),
        lax.all_gather(out_weight, "dp", axis=1, tiled=True),
        lax.all_gather(fc1_weight, "dp", axis=0, tiled=True),
        lax.all_gather(fc2_weight, "dp", axis=1, tiled=True),
    )
    num_lat = latent_tokens.shape[1]
    local_dim = query_key_value_weight.shape[2]
    local_heads = local_dim // HEAD_DIM
    cond_f = cond.astype(jnp.float32)
    silu_cond = jax.nn.silu(cond_f).astype(jnp.bfloat16)
    mod_part = jnp.einsum(
        "bd,dke->bke", silu_cond, modulation_weight, preferred_element_type=jnp.float32
    )
    modulation = lax.all_gather(mod_part, "tensor", axis=2, tiled=True)
    shift_one, scale_one, gate_one, shift_two, scale_two, gate_two = [
        modulation[None, :, member] for member in range(6)
    ]
    block_inputs = latent_tokens.astype(jnp.float32)
    normed_one, recip_one = layer_norm(block_inputs)
    h_one = (normed_one * (1.0 + scale_one) + shift_one).astype(jnp.bfloat16)
    h_one_all = lax.all_gather(h_one, "tensor", axis=0, tiled=True)
    seq_len = h_one_all.shape[0]
    triple = jnp.einsum(
        "sbd,dke->sbke", h_one_all, query_key_value_weight, preferred_element_type=jnp.float32
    ).astype(jnp.bfloat16)
    by_latent = jnp.moveaxis(triple, 1, 0).reshape(num_lat, seq_len, 3, local_heads, HEAD_DIM)
    q_lat = by_latent[:, :, 0]
    k_lat = by_latent[:, :, 1]
    v_lat = by_latent[:, :, 2]
    att_lat, log_total = jax.vmap(attend_one)(q_lat, k_lat, v_lat)
    attended = jnp.moveaxis(att_lat, 0, 1).reshape(seq_len, num_lat, local_dim)
    rows = attended
    branch = lax.psum_scatter(
        jnp.einsum(
            "sbh,hd->sbd", rows, output_projection_weight, preferred_element_type=jnp.float32
        ).astype(jnp.bfloat16),
        "tensor",
        scatter_dimension=0,
        tiled=True,
    ).astype(jnp.float32)
    middle = block_inputs + gate_one * branch
    normed_two, recip_two = layer_norm(middle)
    h_two = (normed_two * (1.0 + scale_two) + shift_two).astype(jnp.bfloat16)
    h_two_all = lax.all_gather(h_two, "tensor", axis=0, tiled=True)
    hidden = jnp.einsum(
        "sbd,df->sbf", h_two_all, first_dense_weight, preferred_element_type=jnp.float32
    )
    active = jax.nn.gelu(hidden, approximate=True).astype(jnp.bfloat16)
    rows = active
    mlp_branch = lax.psum_scatter(
        jnp.einsum(
            "sbf,fd->sbd", rows, second_dense_weight, preferred_element_type=jnp.float32
        ).astype(jnp.bfloat16),
        "tensor",
        scatter_dimension=0,
        tiled=True,
    ).astype(jnp.float32)
    out_block = (middle + gate_two * mlp_branch).astype(jnp.bfloat16)
    cotangent = grad_out.astype(jnp.float32)
    grad_gate_two = jnp.sum(cotangent * mlp_branch, axis=0)
    grad_mlp = (cotangent * gate_two).astype(jnp.bfloat16)
    grad_mlp_all = lax.all_gather(grad_mlp, "tensor", axis=0, tiled=True)
    grad_fc2 = jnp.einsum("sbf,sbd->fd", active, grad_mlp_all, preferred_element_type=jnp.float32)
    grad_active = jnp.einsum(
        "sbd,fd->sbf", grad_mlp_all, second_dense_weight, preferred_element_type=jnp.float32
    )
    gelu_value, gelu_pull = jax.vjp(lambda inner: jax.nn.gelu(inner, approximate=True), hidden)
    grad_hidden = gelu_pull(grad_active)[0].astype(jnp.bfloat16)
    grad_fc1 = jnp.einsum("sbd,sbf->df", h_two_all, grad_hidden, preferred_element_type=jnp.float32)
    mlp_grads = (grad_fc1, grad_fc2)
    rows = grad_hidden
    grad_h_two = lax.psum_scatter(
        jnp.einsum(
            "sbf,df->sbd", rows, first_dense_weight, preferred_element_type=jnp.float32
        ).astype(jnp.bfloat16),
        "tensor",
        scatter_dimension=0,
        tiled=True,
    ).astype(jnp.float32)
    grad_shift_two = jnp.sum(grad_h_two, axis=0)
    grad_scale_two = jnp.sum(grad_h_two * normed_two, axis=0)
    grad_middle = cotangent + norm_back(grad_h_two * (1.0 + scale_two), normed_two, recip_two)
    grad_gate_one = jnp.sum(grad_middle * branch, axis=0)
    grad_branch = (grad_middle * gate_one).astype(jnp.bfloat16)
    grad_branch_all = lax.all_gather(grad_branch, "tensor", axis=0, tiled=True)
    grad_wout = jnp.einsum(
        "sbh,sbd->hd", attended, grad_branch_all, preferred_element_type=jnp.float32
    )
    grad_att = jnp.einsum(
        "sbd,hd->sbh", grad_branch_all, output_projection_weight, preferred_element_type=jnp.float32
    ).astype(jnp.bfloat16)
    grad_att_lat = jnp.moveaxis(grad_att, 1, 0).reshape(num_lat, seq_len, local_heads, HEAD_DIM)
    grad_triple_lat = jax.vmap(attend_back)(q_lat, k_lat, v_lat, grad_att_lat, log_total)
    grad_triple = jnp.moveaxis(grad_triple_lat, 0, 1).reshape(seq_len, num_lat, 3, local_dim)
    grad_wqkv = jnp.einsum(
        "sbd,sbke->dke", h_one_all, grad_triple, preferred_element_type=jnp.float32
    )
    rows = grad_triple
    grad_h_one = lax.psum_scatter(
        jnp.einsum(
            "sbke,dke->sbd", rows, query_key_value_weight, preferred_element_type=jnp.float32
        ).astype(jnp.bfloat16),
        "tensor",
        scatter_dimension=0,
        tiled=True,
    ).astype(jnp.float32)
    grad_shift_one = jnp.sum(grad_h_one, axis=0)
    grad_scale_one = jnp.sum(grad_h_one * normed_one, axis=0)
    grad_input = grad_middle + norm_back(grad_h_one * (1.0 + scale_one), normed_one, recip_one)
    grad_mod_part = jnp.stack(
        [
            grad_shift_one,
            grad_scale_one,
            grad_gate_one,
            grad_shift_two,
            grad_scale_two,
            grad_gate_two,
        ],
        axis=1,
    )
    grad_mod = lax.psum_scatter(
        grad_mod_part.astype(jnp.bfloat16), "tensor", scatter_dimension=2, tiled=True
    )
    grad_wmod = jnp.einsum("bd,bke->dke", silu_cond, grad_mod, preferred_element_type=jnp.float32)
    grad_silu_part = jnp.einsum(
        "bke,dke->bd", grad_mod, modulation_weight, preferred_element_type=jnp.float32
    )
    grad_silu = lax.psum(grad_silu_part, "tensor")
    silu_value, silu_pull = jax.vjp(jax.nn.silu, cond_f)
    grad_condition = silu_pull(grad_silu)[0]
    grad_a, grad_b, grad_c, grad_d, grad_e = (
        lax.psum_scatter(
            grad_wmod.astype(jnp.bfloat16), "dp", scatter_dimension=0, tiled=True
        ).astype(jnp.float32),
        lax.psum_scatter(
            grad_wqkv.astype(jnp.bfloat16), "dp", scatter_dimension=0, tiled=True
        ).astype(jnp.float32),
        lax.psum_scatter(
            grad_wout.astype(jnp.bfloat16), "dp", scatter_dimension=1, tiled=True
        ).astype(jnp.float32),
        lax.psum_scatter(
            mlp_grads[0].astype(jnp.bfloat16), "dp", scatter_dimension=0, tiled=True
        ).astype(jnp.float32),
        lax.psum_scatter(
            mlp_grads[1].astype(jnp.bfloat16), "dp", scatter_dimension=1, tiled=True
        ).astype(jnp.float32),
    )
    return (out_block, grad_input, grad_condition, grad_a, grad_b, grad_c, grad_d, grad_e)


def solution(mesh):
    return jax.shard_map(
        body,
        mesh=mesh,
        in_specs=(
            P("tensor", "dp", None),
            P("dp", None),
            P("dp", None, "tensor"),
            P("dp", None, "tensor"),
            P("tensor", "dp"),
            P("dp", "tensor"),
            P("tensor", "dp"),
            P("tensor", "dp", None),
        ),
        out_specs=(
            P("tensor", "dp", None),
            P("tensor", "dp", None),
            P("dp", None),
            P("dp", None, "tensor"),
            P("dp", None, "tensor"),
            P("tensor", "dp"),
            P("dp", "tensor"),
            P("tensor", "dp"),
        ),
        check_vma=False,
    )
```

profile of v0, /device:TPU:0, one launch (start us, length us, event | category | flops | bytes accessed | tf_op | source)
XLA Modules:
  0.0 1197.6 jit_solution(11897335591764480186)
XLA Ops:
  11.3 79.4 %all-gather.10.cloned.1.call-done = bf16[1152,6,576]{2,0,1:T(8,128)(2,1)} async-done(((bf16[72,6,576]{2,0,1:T(8,128)(2,1)}), bf16[1152,6,576]{2,0,1:T(8,128)(2,1)}) %all-gather.10.cloned.1.call-update) | async-done | bytes 7962640 | tf_op jit(solution)/shard_map/all_gather | solution.py:68
  95.8 16.2 %all_gather.31 = f32[2,6,1152]{1,0,2:T(2,128)S(1)} all-gather(f32[2,6,576]{1,0,2:T(2,128)S(1)} %copy.78), channel_id=1, replica_groups=mesh['dp'=16,'tensor'=2] {'tensor'}, dimensions={2}, use_global_device_ids=true | all-gather | bytes 82944 | tf_op jit(solution)/shard_map/all_gather | solution.py:82
  125.0 17.9 %all-gather.14.cloned.1.call-done = bf16[1152,3,576]{2,0,1:T(8,128)(2,1)} async-done(((bf16[72,3,576]{2,0,1:T(8,128)(2,1)}), bf16[1152,3,576]{2,0,1:T(8,128)(2,1)}) %all-gather.14.cloned.1.call-update) | async-done | bytes 3981328 | tf_op jit(solution)/shard_map/all_gather | solution.py:69
  142.9 36.7 %all-gather.12.cloned.1.call-done = bf16[512,2,1152]{2,0,1:T(8,128)(2,1)} async-done(((bf16[256,2,1152]{2,0,1:T(8,128)(2,1)}), bf16[512,2,1152]{2,0,1:T(8,128)(2,1)}) %all-gather.12.cloned.1.call-update) | async-done | bytes 2359312 | tf_op jit(solution)/shard_map/all_gather | solution.py:89
  233.1 27.0 %reduce-scatter.17.cloned.1.call-done = bf16[256,2,1152]{2,0,1:T(8,128)(2,1)} async-done(((bf16[512,2,1152]{2,0,1:T(8,128)(2,1)}), bf16[256,2,1152]{2,0,1:T(8,128)(2,1)}) %reduce-scatter.17.cloned.1.call-update) | async-done | bytes 1179664 | tf_op jit(solution)/shard_map/reduce_scatter | solution.py:101
  269.8 49.0 %all-gather.20.cloned.1.call-done = bf16[1152,2304]{1,0:T(8,128)(2,1)} async-done(((bf16[72,2304]{1,0:T(8,128)(2,1)}), bf16[1152,2304]{1,0:T(8,128)(2,1)}) %all-gather.20.cloned.1.call-update) | async-done | bytes 5308432 | tf_op jit(solution)/shard_map/all_gather | solution.py:71
  318.8 36.9 %all-gather.18.cloned.1.call-done = bf16[512,2,1152]{2,0,1:T(8,128)(2,1)} async-done(((bf16[256,2,1152]{2,0,1:T(8,128)(2,1)}), bf16[512,2,1152]{2,0,1:T(8,128)(2,1)}) %all-gather.18.cloned.1.call-update) | async-done | bytes 2359312 | tf_op jit(solution)/shard_map/all_gather | solution.py:112
  355.6 11.9 fusion.21
  367.5 47.0 %all-gather.22.cloned.1.call-done = bf16[2304,1152]{0,1:T(8,128)(2,1)} async-done(((bf16[2304,72]{0,1:T(8,128)(2,1)}), bf16[2304,1152]{0,1:T(8,128)(2,1)}) %all-gather.22.cloned.1.call-update) | async-done | bytes 5308432 | tf_op jit(solution)/shard_map/all_gather | solution.py:72
  414.4 36.9 %all-gather.24.cloned.1.call-done = bf16[512,2,1152]{2,0,1:T(8,128)(2,1)} async-done(((bf16[256,2,1152]{2,0,1:T(8,128)(2,1)}), bf16[512,2,1152]{2,0,1:T(8,128)(2,1)}) %all-gather.24.cloned.1.call-update) | async-done | bytes 2359312 | tf_op jit(solution)/shard_map/all_gather | solution.py:130
  451.3 14.0 %fusion.10 = bf16[512,2,2304]{2,0,1:T(8,128)(2,1)S(1)} fusion(f32[512,2,2304]{2,0,1:T(8,128)} %fusion.21, bf16[512,2,1152]{2,0,1:T(8,128)(2,1)} %all-gather.24.cloned.1.call-done, bf16[2304,1152]{0,1:T(8,128)(2,1)} %all-gather.22.cloned.1.call-done), kind=kOutput, calls=%fused_computation.21 | convolution fusion | flops 5483003904 | bytes 21823488 | tf_op jit(solution)/shard_map/sbd,fd->sbf/dot_general | solution.py:132
  477.5 34.8 %reduce-scatter.21.cloned.1.call-done = bf16[256,2,1152]{2,0,1:T(8,128)(2,1)} async-done(((bf16[512,2,1152]{2,0,1:T(8,128)(2,1)}), bf16[256,2,1152]{2,0,1:T(8,128)(2,1)}) %reduce-scatter.21.cloned.1.call-update) | async-done | bytes 1179664 | tf_op jit(solution)/shard_map/reduce_scatter | solution.py:140
  520.1 34.6 %all-gather.26.cloned.1.call-done = bf16[512,2,1152]{2,0,1:T(8,128)(2,1)} async-done(((bf16[256,2,1152]{2,0,1:T(8,128)(2,1)}), bf16[512,2,1152]{2,0,1:T(8,128)(2,1)}) %all-gather.26.cloned.1.call-update) | async-done | bytes 2359312 | tf_op jit(solution)/shard_map/all_gather | solution.py:153
  577.6 11.8 multiply_convert_fusion
  605.5 13.1 %fusion.30 = bf16[512,2,1152]{2,0,1:T(8,128)(2,1)} fusion(bf16[2304,1152]{0,1:T(8,128)(2,1)} %all-gather.22.cloned.1.call-done, f32[512,2,2304]{2,0,1:T(8,128)} %fusion.21), kind=kOutput, calls=%fused_computation.41 | convolution fusion | flops 5458231296 | bytes 17104896 | tf_op jit(solution)/shard_map/sbf,fd->sbd/dot_general | solution.py:119
  619.6 20.4 %reduce-scatter.23.cloned.1.call-done = bf16[256,2,1152]{2,0,1:T(8,128)(2,1)} async-done(((bf16[512,2,1152]{2,0,1:T(8,128)(2,1)}), bf16[256,2,1152]{2,0,1:T(8,128)(2,1)}) %reduce-scatter.23.cloned.1.call-update) | async-done | bytes 1179664 | tf_op jit(solution)/shard_map/reduce_scatter | solution.py:167
  643.3 34.3 %reduce-scatter.19.cloned.1.call-done = bf16[256,2,1152]{2,0,1:T(8,128)(2,1)} async-done(((bf16[512,2,1152]{2,0,1:T(8,128)(2,1)}), bf16[256,2,1152]{2,0,1:T(8,128)(2,1)}) %reduce-scatter.19.cloned.1.call-update) | async-done | bytes 1179664 | tf_op jit(solution)/shard_map/reduce_scatter | solution.py:118
  731.0 18.2 %copy.115 = bf16[1152,3,576]{2,1,0:T(4,128)(2,1)} copy(bf16[1152,3,576]{2,0,1:T(8,128)(2,1)S(1)} %bitcast_convert_fusion) | data formatting | bytes 7962624
  749.2 12.3 %reshape.122 = bf16[1152,1728]{1,0:T(8,128)(2,1)} reshape(bf16[1152,3,576]{2,1,0:T(4,128)(2,1)} %copy.115) | data formatting | bytes 7962624
  775.5 15.0 %reduce-scatter.27.cloned.1.call-done = bf16[2304,72]{0,1:T(8,128)(2,1)} async-done(((bf16[2304,1152]{0,1:T(8,128)(2,1)}), bf16[2304,72]{0,1:T(8,128)(2,1)}) %reduce-scatter.27.cloned.1.call-update) | async-done | bytes 331792 | tf_op jit(solution)/shard_map/reduce_scatter | solution.py:212
  792.4 80.7 %reduce-scatter.25.cloned.1.call-done = bf16[72,2304]{1,0:T(8,128)(2,1)} async-done(((bf16[1152,2304]{1,0:T(8,128)(2,1)}), bf16[72,2304]{1,0:T(8,128)(2,1)}) %reduce-scatter.25.cloned.1.call-update) | async-done | bytes 331792 | tf_op jit(solution)/shard_map/reduce_scatter | solution.py:209
  874.9 60.3 %reduce-scatter.33.cloned.1.call-done = bf16[576,72]{0,1:T(8,128)(2,1)} async-done(((bf16[576,1152]{0,1:T(8,128)(2,1)}), bf16[576,72]{0,1:T(8,128)(2,1)}) %reduce-scatter.33.cloned.1.call-update) | async-done | bytes 82960
  958.9 51.1 %reduce-scatter.31.cloned.1.call-done = bf16[72,1728]{1,0:T(8,128)(2,1)} async-done(((bf16[1152,1728]{1,0:T(8,128)(2,1)}), bf16[72,1728]{1,0:T(8,128)(2,1)}) %reduce-scatter.31.cloned.1.call-update) | async-done | bytes 248848
  1012.0 176.8 %all-reduce.4.cloned.1.call-done = bf16[1152,6,576]{2,0,1:T(8,128)(2,1)} async-done(((bf16[1152,6,576]{2,0,1:T(8,128)(2,1)}), bf16[1152,6,576]{2,0,1:T(8,128)(2,1)}) %all-reduce.4.cloned.1.call-update) | async-done | bytes 7962640
  (162 shorter events, 246.2 us)
Async XLA Ops:
  7.2 83.5 %copy-start.18 = (bf16[2,1152]{1,0:T(2,128)(2,1)S(1)}, bf16[2,1152]{1,0:T(2,128)(2,1)}, u32[]{:S(2)}) copy-start(bf16[2,1152]{1,0:T(2,128)(2,1)} %param.9) | copy-start | bytes 13828
  7.2 83.5 %all-gather.10.cloned.1.call-start = ((), (), s32[]{:S(2)}) async-start(), calls=%async_computation.9 | async-start | bytes 9400320 | tf_op jit(solution)/shard_map/all_gather | solution.py:68
  7.9 134.9 %all-gather.14.cloned.1.call-start = ((), (), s32[]{:S(2)}) async-start(), calls=%async_computation.11 | async-start | bytes 4700160 | tf_op jit(solution)/shard_map/all_gather | solution.py:69
  8.7 170.9 %all-gather.12.cloned.1.call-start = ((), (), s32[]{:S(2)}) async-start(), calls=%async_computation.10 | async-start | bytes 3538944 | tf_op jit(solution)/shard_map/all_gather | solution.py:89
  10.2 111.4 %copy-start.17 = (f32[256,2]{0,1:T(2,128)}, f32[256,2]{0,1:T(2,128)S(1)}, u32[]{:S(2)}) copy-start(f32[256,2]{0,1:T(2,128)S(1)} %broadcast_multiply_fusion.5) | copy-start | bytes 6148
  124.3 96.7 %all-gather.16.cloned.1.call-start = ((), (), s32[]{:S(2)}) async-start(), calls=%async_computation.12 | async-start | bytes 1566720 | tf_op jit(solution)/shard_map/all_gather | solution.py:70
  124.9 135.2 %reduce-scatter.17.cloned.1.call-start = ((), (), s32[]{:S(2)}) async-start(), calls=%async_computation.13 | async-start | bytes 3538944 | tf_op jit(solution)/shard_map/reduce_scatter | solution.py:101
  187.4 15.9 %copy-start.4 = (bf16[512,2,3,576]{0,3,2,1:T(8,128)(2,1)}, bf16[512,2,3,576]{0,3,2,1:T(8,128)(2,1)S(1)}, u32[]{:S(2)}) copy-start(bf16[512,2,3,576]{0,3,2,1:T(8,128)(2,1)S(1)} %fusion.46) | copy-start | bytes 10616836
  203.3 9.1 copy-start.15
  226.4 92.4 %all-gather.20.cloned.1.call-start = ((), (), s32[]{:S(2)}) async-start(), calls=%async_computation.15 | async-start | bytes 5640192 | tf_op jit(solution)/shard_map/all_gather | solution.py:71
  227.0 128.6 %all-gather.18.cloned.1.call-start = ((), (), s32[]{:S(2)}) async-start(), calls=%async_computation.14 | async-start | bytes 3538944 | tf_op jit(solution)/shard_map/all_gather | solution.py:112
  264.8 149.6 %all-gather.22.cloned.1.call-start = ((), (), s32[]{:S(2)}) async-start(), calls=%async_computation.16 | async-start | bytes 5640192 | tf_op jit(solution)/shard_map/all_gather | solution.py:72
  265.6 185.7 %all-gather.24.cloned.1.call-start = ((), (), s32[]{:S(2)}) async-start(), calls=%async_computation.18 | async-start | bytes 3538944 | tf_op jit(solution)/shard_map/all_gather | solution.py:130
  269.7 242.6 %reduce-scatter.21.cloned.1.call-start = ((), (), s32[]{:S(2)}) async-start(), calls=%async_computation.19 | async-start | bytes 3538944 | tf_op jit(solution)/shard_map/reduce_scatter | solution.py:140
  477.5 77.2 %all-gather.26.cloned.1.call-start = ((), (), s32[]{:S(2)}) async-start(), calls=%async_computation.20 | async-start | bytes 3538944 | tf_op jit(solution)/shard_map/all_gather | solution.py:153
  518.5 121.5 %reduce-scatter.23.cloned.1.call-start = ((), (), s32[]{:S(2)}) async-start(), calls=%async_computation.21 | async-start | bytes 3538944 | tf_op jit(solution)/shard_map/reduce_scatter | solution.py:167
  605.1 72.5 %reduce-scatter.19.cloned.1.call-start = ((), (), s32[]{:S(2)}) async-start(), calls=%async_computation.17 | async-start | bytes 3538944 | tf_op jit(solution)/shard_map/reduce_scatter | solution.py:118
  618.7 143.1 %reduce-scatter.29.cloned.1.call-start = ((), (), s32[]{:S(2)}) async-start(), calls=%async_computation.24 | async-start | bytes 442368
  694.8 95.7 %reduce-scatter.27.cloned.1.call-start = ((), (), s32[]{:S(2)}) async-start(), calls=%async_computation.23 | async-start | bytes 5640192 | tf_op jit(solution)/shard_map/reduce_scatter | solution.py:212
  706.3 166.8 %reduce-scatter.25.cloned.1.call-start = ((), (), s32[]{:S(2)}) async-start(), calls=%async_computation.22 | async-start | bytes 5640192 | tf_op jit(solution)/shard_map/reduce_scatter | solution.py:209
  717.1 218.1 %reduce-scatter.33.cloned.1.call-start = ((), (), s32[]{:S(2)}) async-start(), calls=%async_computation.27 | async-start | bytes 1566720
  722.7 287.3 %reduce-scatter.31.cloned.1.call-start = ((), (), s32[]{:S(2)}) async-start(), calls=%async_computation.25 | async-start | bytes 4386816
  761.5 427.2 %all-reduce.4.cloned.1.call-start = ((), (), s32[]{:S(2)}) async-start(), calls=%async_computation.26 | async-start | bytes 17694720
  946.8 11.4 copy-start.19
  (20 other events, 65.9 us)
Sparse Core Ops, SparseCore 0:
  10.2 80.4 all-gather.9
  92.9 49.9 all-gather.13
  145.0 34.5 all-gather.11
  181.6 39.3 all-gather.15
  226.5 33.5 reduce-scatter.16
  262.4 56.3 all-gather.19
  321.0 34.6 all-gather.17
  358.0 56.3 all-gather.21
  416.6 34.6 all-gather.23
  477.6 34.6 reduce-scatter.20
  518.6 36.0 all-gather.25
  605.2 34.7 reduce-scatter.22
  642.9 34.6 reduce-scatter.18
  694.9 12.0 reduce-scatter.28
  710.9 79.5 reduce-scatter.26
  794.4 78.6 reduce-scatter.24
  877.3 57.8 reduce-scatter.32
  939.0 70.9 reduce-scatter.30
  1013.7 175.0 all-reduce.3
where the time goes:
time: 1210 us; the launch traced here: 1200 us
  waiting for transfers between devices  851 us (70%)
  matrix products  168 us (14%)
  local copies, waits for them, and re-layouts  77.3 us (6%)
  other arithmetic  63.1 us (5%)
  blocking collectives  21.2 us (2%)
  between operations  15.2 us (1%)
    unnamed x23, waiting for transfers between devices  292 us
    reduce_scatter x1, waiting for transfers between devices, body(): lax.psum_scatter(mlp_grads[0].astype(jnp.bfloat16), 'dp', scatter_dimensi...  80.7 us
    all_gather x1, waiting for transfers between devices, body(): lax.all_gather(mod_weight, 'dp', axis=0, tiled=True)  79.4 us
    unnamed x67, local copies, waits for them, and re-layouts  62.6 us
    all_gather x1, waiting for transfers between devices, body(): lax.all_gather(fc1_weight, 'dp', axis=0, tiled=True)  49 us
    all_gather x1, waiting for transfers between devices, body(): lax.all_gather(fc2_weight, 'dp', axis=1, tiled=True)  47 us
    all_gather x1, waiting for transfers between devices, body(): grad_mlp_all = lax.all_gather(grad_mlp, 'tensor', axis=0, tiled=True)  36.9 us
    all_gather x1, waiting for transfers between devices, body(): h_two_all = lax.all_gather(h_two, 'tensor', axis=0, tiled=True)  36.9 us
  transfers between devices with their start and end apart: 19, of which 18 were waited for; matrix products, arithmetic and copies ran while one was open for 17% of the time, Pallas kernels for 0%

commit v1 on v0

--- a/solution.py
+++ b/solution.py
@@ -57,15 +57,32 @@
     return jnp.stack([grad_q, grad_k, grad_v], axis=1).astype(jnp.bfloat16)
 
 
+def spread(rows):
+    size = lax.axis_size("tensor")
+    if size == 2:
+        other = lax.ppermute(rows, "tensor", [(0, 1), (1, 0)])
+        return jnp.concatenate([rows, other], axis=0)
+    return lax.all_gather(rows, "tensor", axis=0, tiled=True)
+
+
+def shrink(terms):
+    size = lax.axis_size("tensor")
+    if size == 2:
+        half = terms.shape[0] // 2
+        other = lax.ppermute(terms[half:].astype(jnp.bfloat16), "tensor", [(0, 1), (1, 0)])
+        return terms[:half].astype(jnp.float32) + other.astype(jnp.float32)
+    return lax.psum_scatter(
+        terms.astype(jnp.bfloat16), "tensor", scatter_dimension=0, tiled=True
+    ).astype(jnp.float32)
+
+
 def body(latent_tokens, cond, mod_weight, qkv_weight, out_weight, fc1_weight, fc2_weight, grad_out):
     (
-        modulation_weight,
         query_key_value_weight,
         output_projection_weight,
         first_dense_weight,
         second_dense_weight,
     ) = (
-        lax.all_gather(mod_weight, "dp", axis=0, tiled=True),
         lax.all_gather(qkv_weight, "dp", axis=0, tiled=True),
         lax.all_gather(out_weight, "dp", axis=1, tiled=True),
         lax.all_gather(fc1_weight, "dp", axis=0, tiled=True),
@@ -76,8 +93,16 @@
     local_heads = local_dim // HEAD_DIM
     cond_f = cond.astype(jnp.float32)
     silu_cond = jax.nn.silu(cond_f).astype(jnp.bfloat16)
-    mod_part = jnp.einsum(
-        "bd,dke->bke", silu_cond, modulation_weight, preferred_element_type=jnp.float32
+    silu_all = lax.all_gather(silu_cond, "dp", axis=0, tiled=True)
+    mod_rows = mod_weight.shape[0]
+    silu_rows = lax.dynamic_slice_in_dim(
+        silu_all, lax.axis_index("dp") * mod_rows, mod_rows, axis=1
+    )
+    mod_part = lax.psum_scatter(
+        jnp.einsum("bd,dke->bke", silu_rows, mod_weight, preferred_element_type=jnp.float32),
+        "dp",
+        scatter_dimension=0,
+        tiled=True,
     )
     modulation = lax.all_gather(mod_part, "tensor", axis=2, tiled=True)
     shift_one, scale_one, gate_one, shift_two, scale_two, gate_two = [
@@ -86,7 +111,7 @@
     block_inputs = latent_tokens.astype(jnp.float32)
     normed_one, recip_one = layer_norm(block_inputs)
     h_one = (normed_one * (1.0 + scale_one) + shift_one).astype(jnp.bfloat16)
-    h_one_all = lax.all_gather(h_one, "tensor", axis=0, tiled=True)
+    h_one_all = spread(h_one)
     seq_len = h_one_all.shape[0]
     triple = jnp.einsum(
         "sbd,dke->sbke", h_one_all, query_key_value_weight, preferred_element_type=jnp.float32
@@ -98,36 +123,30 @@
     att_lat, log_total = jax.vmap(attend_one)(q_lat, k_lat, v_lat)
     attended = jnp.moveaxis(att_lat, 0, 1).reshape(seq_len, num_lat, local_dim)
     rows = attended
-    branch = lax.psum_scatter(
+    branch = shrink(
         jnp.einsum(
             "sbh,hd->sbd", rows, output_projection_weight, preferred_element_type=jnp.float32
-        ).astype(jnp.bfloat16),
-        "tensor",
-        scatter_dimension=0,
-        tiled=True,
-    ).astype(jnp.float32)
+        )
+    )
     middle = block_inputs + gate_one * branch
     normed_two, recip_two = layer_norm(middle)
     h_two = (normed_two * (1.0 + scale_two) + shift_two).astype(jnp.bfloat16)
-    h_two_all = lax.all_gather(h_two, "tensor", axis=0, tiled=True)
+    h_two_all = spread(h_two)
     hidden = jnp.einsum(
         "sbd,df->sbf", h_two_all, first_dense_weight, preferred_element_type=jnp.float32
     )
     active = jax.nn.gelu(hidden, approximate=True).astype(jnp.bfloat16)
     rows = active
-    mlp_branch = lax.psum_scatter(
+    mlp_branch = shrink(
         jnp.einsum(
             "sbf,fd->sbd", rows, second_dense_weight, preferred_element_type=jnp.float32
-        ).astype(jnp.bfloat16),
-        "tensor",
-        scatter_dimension=0,
-        tiled=True,
-    ).astype(jnp.float32)
+        )
+    )
     out_block = (middle + gate_two * mlp_branch).astype(jnp.bfloat16)
     cotangent = grad_out.astype(jnp.float32)
     grad_gate_two = jnp.sum(cotangent * mlp_branch, axis=0)
     grad_mlp = (cotangent * gate_two).astype(jnp.bfloat16)
-    grad_mlp_all = lax.all_gather(grad_mlp, "tensor", axis=0, tiled=True)
+    grad_mlp_all = spread(grad_mlp)
     grad_fc2 = jnp.einsum("sbf,sbd->fd", active, grad_mlp_all, preferred_element_type=jnp.float32)
     grad_active = jnp.einsum(
         "sbd,fd->sbf", grad_mlp_all, second_dense_weight, preferred_element_type=jnp.float32
@@ -137,20 +156,17 @@
     grad_fc1 = jnp.einsum("sbd,sbf->df", h_two_all, grad_hidden, preferred_element_type=jnp.float32)
     mlp_grads = (grad_fc1, grad_fc2)
     rows = grad_hidden
-    grad_h_two = lax.psum_scatter(
+    grad_h_two = shrink(
         jnp.einsum(
             "sbf,df->sbd", rows, first_dense_weight, preferred_element_type=jnp.float32
-        ).astype(jnp.bfloat16),
-        "tensor",
-        scatter_dimension=0,
-        tiled=True,
-    ).astype(jnp.float32)
+        )
+    )
     grad_shift_two = jnp.sum(grad_h_two, axis=0)
     grad_scale_two = jnp.sum(grad_h_two * normed_two, axis=0)
     grad_middle = cotangent + norm_back(grad_h_two * (1.0 + scale_two), normed_two, recip_two)
     grad_gate_one = jnp.sum(grad_middle * branch, axis=0)
     grad_branch = (grad_middle * gate_one).astype(jnp.bfloat16)
-    grad_branch_all = lax.all_gather(grad_branch, "tensor", axis=0, tiled=True)
+    grad_branch_all = spread(grad_branch)
     grad_wout = jnp.einsum(
         "sbh,sbd->hd", attended, grad_branch_all, preferred_element_type=jnp.float32
     )
@@ -164,14 +180,11 @@
         "sbd,sbke->dke", h_one_all, grad_triple, preferred_element_type=jnp.float32
     )
     rows = grad_triple
-    grad_h_one = lax.psum_scatter(
+    grad_h_one = shrink(
         jnp.einsum(
             "sbke,dke->sbd", rows, query_key_value_weight, preferred_element_type=jnp.float32
-        ).astype(jnp.bfloat16),
-        "tensor",
-        scatter_dimension=0,
-        tiled=True,
-    ).astype(jnp.float32)
+        )
+    )
     grad_shift_one = jnp.sum(grad_h_one, axis=0)
     grad_scale_one = jnp.sum(grad_h_one * normed_one, axis=0)
     grad_input = grad_middle + norm_back(grad_h_one * (1.0 + scale_one), normed_one, recip_one)
@@ -187,19 +200,20 @@
         axis=1,
     )
     grad_mod = lax.psum_scatter(
-        grad_mod_part.astype(jnp.bfloat16), "tensor", scatter_dimension=2, tiled=True
-    )
-    grad_wmod = jnp.einsum("bd,bke->dke", silu_cond, grad_mod, preferred_element_type=jnp.float32)
+        grad_mod_part, "tensor", scatter_dimension=2, tiled=True
+    ).astype(jnp.bfloat16)
+    grad_mod_all = lax.all_gather(grad_mod, "dp", axis=0, tiled=True)
+    grad_wmod = jnp.einsum(
+        "bd,bke->dke", silu_rows, grad_mod_all, preferred_element_type=jnp.float32
+    )
     grad_silu_part = jnp.einsum(
-        "bke,dke->bd", grad_mod, modulation_weight, preferred_element_type=jnp.float32
-    )
+        "bke,dke->bd", grad_mod_all, mod_weight, preferred_element_type=jnp.float32
+    )
+    grad_silu_part = lax.all_to_all(grad_silu_part, "dp", split_axis=0, concat_axis=1, tiled=True)
     grad_silu = lax.psum(grad_silu_part, "tensor")
     silu_value, silu_pull = jax.vjp(jax.nn.silu, cond_f)
     grad_condition = silu_pull(grad_silu)[0]
-    grad_a, grad_b, grad_c, grad_d, grad_e = (
-        lax.psum_scatter(
-            grad_wmod.astype(jnp.bfloat16), "dp", scatter_dimension=0, tiled=True
-        ).astype(jnp.float32),
+    grad_b, grad_c, grad_d, grad_e = (
         lax.psum_scatter(
             grad_wqkv.astype(jnp.bfloat16), "dp", scatter_dimension=0, tiled=True
         ).astype(jnp.float32),
@@ -213,7 +227,7 @@
             mlp_grads[1].astype(jnp.bfloat16), "dp", scatter_dimension=1, tiled=True
         ).astype(jnp.float32),
     )
-    return (out_block, grad_input, grad_condition, grad_a, grad_b, grad_c, grad_d, grad_e)
+    return (out_block, grad_input, grad_condition, grad_wmod, grad_b, grad_c, grad_d, grad_e)
 
 
 def solution(mesh):

time: 1210 us -> 850 us (0.70)
  waiting for transfers between devices: 851 us -> 486 us
  blocking collectives: 21.2 us -> 63.4 us
  matrix products: 168 us -> 142 us
  other arithmetic: 63.1 us -> 45.6 us
  starting transfers between devices: 1.74 us -> 14.2 us
    all_gather x5 -> x0, waiting for transfers between devices: 224 us -> none  [the longest x1 79.4 us: body(): lax.all_gather(mod_weight, 'dp', axis=0, tiled=True)]
    ppermute x0 -> x8, waiting for transfers between devices: none -> 171 us  [the longest x4 85.5 us: shrink(): lax.ppermute(terms[half:].astype(jnp.bfloat16), 'tensor', [(0, 1), (1, 0)])]
    unnamed x23 -> x14, waiting for transfers between devices: 292 us -> 160 us
    reduce_scatter x4 -> x0, waiting for transfers between devices: 117 us -> none  [the longest x1 34.8 us: body(): lax.psum_scatter(jnp.einsum('sbf,df->sbd', rows, first_dense_weight, pref...]
    all_gather x1, waiting for transfers between devices: 49 us -> 0.01 us  [body(): lax.all_gather(fc1_weight, 'dp', axis=0, tiled=True)]
    all_gather x0 -> x2, blocking collectives: none -> 43.4 us  [the longest x1 23.3 us: body(): silu_all = lax.all_gather(silu_cond, 'dp', axis=0, tiled=True)]
    reduce_scatter x1, waiting for transfers between devices: 15 us -> 43.4 us  [body(): lax.psum_scatter(mlp_grads[1].astype(jnp.bfloat16), 'dp', scatter_dimensi...]
    all_gather x1, waiting for transfers between devices: 47 us -> 19.8 us  [body(): lax.all_gather(fc2_weight, 'dp', axis=1, tiled=True)]
  transfers between devices with their start and end apart: 19 -> 19, of which waited for: 18 -> 15; matrix products, arithmetic and copies ran while one was open for 17% -> 21% of each run, Pallas kernels for 0% -> 0%
where the time goes in v1:
time: 850 us; the launch traced here: 842 us
  waiting for transfers between devices  486 us (57%)
  matrix products  142 us (17%)
  local copies, waits for them, and re-layouts  74.3 us (9%)
  blocking collectives  63.4 us (7%)
  other arithmetic  45.6 us (5%)
  between operations  15.7 us (2%)
  starting transfers between devices  14.2 us (2%)
    unnamed x14, waiting for transfers between devices  160 us
    ppermute x4, waiting for transfers between devices, shrink(): lax.ppermute(terms[half:].astype(jnp.bfloat16), 'tensor', [(0, 1), (1, 0)])  85.5 us
    ppermute x4, waiting for transfers between devices, spread(): other = lax.ppermute(rows, 'tensor', [(0, 1), (1, 0)])  85.3 us
    reduce_scatter x1, waiting for transfers between devices, body(): lax.psum_scatter(mlp_grads[0].astype(jnp.bfloat16), 'dp', scatter_dimensi...  81.3 us
    unnamed x91, local copies, waits for them, and re-layouts  58.5 us
    reduce_scatter x1, waiting for transfers between devices, body(): lax.psum_scatter(mlp_grads[1].astype(jnp.bfloat16), 'dp', scatter_dimensi...  43.4 us
    all_gather x1, blocking collectives, body(): silu_all = lax.all_gather(silu_cond, 'dp', axis=0, tiled=True)  23.3 us
    all_gather x1, blocking collectives, body(): grad_mod_all = lax.all_gather(grad_mod, 'dp', axis=0, tiled=True)  20.1 us
  transfers between devices with their start and end apart: 19, of which 15 were waited for; matrix products, arithmetic and copies ran while one was open for 21% of the time, Pallas kernels for 0%

profile of v1, /device:TPU:0, one launch (start us, length us, event | category | flops | bytes accessed | tf_op | source)
XLA Modules:
  0.0 841.6 jit_solution(9768791245603306076)
XLA Ops:
  8.1 23.3 %all-gather = bf16[16,2,1152]{2,1,0:T(2,128)(2,1)S(1)} all-gather(bf16[1,2,1152]{2,1,0:T(2,128)(2,1)S(1)} %fusion.81), channel_id=1, replica_groups=mesh['dp'=16,'tensor'=2] {'dp'}, dimensions={0}, use_global_device_ids=true | all-gather | bytes 78336 | tf_op jit(solution)/shard_map/all_gather | solution.py:96
  36.6 84.5 %all-reduce.4.cloned.1.call-done = f32[32,6,576]{2,0,1:T(8,128)} async-done(((f32[32,6,576]{2,0,1:T(8,128)}), f32[32,6,576]{2,0,1:T(8,128)}) %all-reduce.4.cloned.1.call-update) | async-done | bytes 442384
  122.3 14.9 %all_gather.22 = f32[2,6,1152]{1,0,2:T(2,128)S(1)} all-gather(f32[2,6,576]{1,0,2:T(2,128)S(1)} %copy.87), channel_id=1, replica_groups=mesh['dp'=16,'tensor'=2] {'tensor'}, dimensions={2}, use_global_device_ids=true | all-gather | bytes 82944 | tf_op jit(solution)/shard_map/all_gather | solution.py:107
  149.7 24.5 %collective-permute-done = bf16[256,2,1152]{2,0,1:T(8,128)(2,1)S(1)} collective-permute-done((bf16[256,2,1152]{2,0,1:T(8,128)(2,1)S(1)}, bf16[256,2,1152]{2,0,1:T(8,128)(2,1)S(1)}, u32[]{:S(2)}, u32[]{:S(2)}) %collective-permute-start) | collective-permute-done | bytes 1179680 | tf_op jit(solution)/shard_map/ppermute | solution.py:63
  227.0 22.7 %collective-permute-done.1 = bf16[256,2,1152]{2,0,1:T(8,128)(2,1)S(1)} collective-permute-done((bf16[256,2,1152]{2,0,1:T(8,128)(2,1)}, bf16[256,2,1152]{2,0,1:T(8,128)(2,1)S(1)}, u32[]{:S(2)}, u32[]{:S(2)}) %collective-permute-start.1) | collective-permute-done | bytes 1179680 | tf_op jit(solution)/shard_map/ppermute | solution.py:72
  261.5 23.1 %collective-permute-done.2 = bf16[256,2,1152]{2,0,1:T(8,128)(2,1)} collective-permute-done((bf16[256,2,1152]{2,0,1:T(8,128)(2,1)}, bf16[256,2,1152]{2,0,1:T(8,128)(2,1)}, u32[]{:S(2)}, u32[]{:S(2)}) %collective-permute-start.2) | collective-permute-done | bytes 1179680 | tf_op jit(solution)/shard_map/ppermute | solution.py:63
  284.7 11.9 %fusion.21 = f32[512,2,2304]{2,0,1:T(8,128)} fusion(bf16[1152,2304]{1,0:T(8,128)(2,1)} %all-gather.10.cloned.1.call-done, bf16[256,2,1152]{2,0,1:T(8,128)(2,1)} %collective-permute-done.2, bf16[256,2,1152]{2,0,1:T(8,128)(2,1)} %add_convert_fusion.1), kind=kOutput, calls=%fused_computation.32 | convolution fusion | flops 5440536576 | bytes 17104896 | tf_op jit(solution)/shard_map/sbd,df->sbf/dot_general | solution.py:135
  296.6 11.9 %collective-permute-done.4 = bf16[256,2,1152]{2,0,1:T(8,128)(2,1)} collective-permute-done((bf16[256,2,1152]{2,0,1:T(8,128)(2,1)}, bf16[256,2,1152]{2,0,1:T(8,128)(2,1)}, u32[]{:S(2)}, u32[]{:S(2)}) %collective-permute-start.4) | collective-permute-done | bytes 1179680 | tf_op jit(solution)/shard_map/ppermute | solution.py:63
  308.5 19.8 %all-gather.12.cloned.1.call-done = bf16[2304,1152]{0,1:T(8,128)(2,1)} async-done(((bf16[2304,72]{0,1:T(8,128)(2,1)}), bf16[2304,1152]{0,1:T(8,128)(2,1)}) %all-gather.12.cloned.1.call-update) | async-done | bytes 5308432 | tf_op jit(solution)/shard_map/all_gather | solution.py:89
  328.3 15.0 %fusion.10 = bf16[512,2,2304]{2,0,1:T(8,128)(2,1)S(1)} fusion(f32[512,2,2304]{2,0,1:T(8,128)} %fusion.21, bf16[2304,1152]{0,1:T(8,128)(2,1)} %all-gather.12.cloned.1.call-done, bf16[256,2,1152]{2,0,1:T(8,128)(2,1)} %collective-permute-done.4, bf16[256,2,1152]{2,0,1:T(8,128)(2,1)} %fusion.48), kind=kOutput, calls=%fused_computation.20 | convolution fusion | flops 5487722496 | bytes 21823488 | tf_op jit(solution)/shard_map/sbd,fd->sbf/dot_general | solution.py:151
  352.3 12.3 %fusion.17 = f32[512,2,1152]{2,0,1:T(8,128)S(1)} fusion(bf16[2304,1152]{0,1:T(8,128)(2,1)} %all-gather.12.cloned.1.call-done, f32[512,2,2304]{2,0,1:T(8,128)} %fusion.21), kind=kOutput, calls=%fused_computation.28 | convolution fusion | flops 5457051648 | bytes 19464192 | tf_op jit(solution)/shard_map/sbf,fd->sbd/dot_general | solution.py:141
  365.4 14.4 %collective-permute-done.5 = bf16[256,2,1152]{2,0,1:T(8,128)(2,1)S(1)} collective-permute-done((bf16[256,2,1152]{2,0,1:T(8,128)(2,1)}, bf16[256,2,1152]{2,0,1:T(8,128)(2,1)S(1)}, u32[]{:S(2)}, u32[]{:S(2)}) %collective-permute-start.5) | collective-permute-done | bytes 1179680 | tf_op jit(solution)/shard_map/ppermute | solution.py:72
  381.1 23.4 %collective-permute-done.3 = bf16[256,2,1152]{2,0,1:T(8,128)(2,1)S(1)} collective-permute-done((bf16[256,2,1152]{2,0,1:T(8,128)(2,1)S(1)}, bf16[256,2,1152]{2,0,1:T(8,128)(2,1)S(1)}, u32[]{:S(2)}, u32[]{:S(2)}) %collective-permute-start.3) | collective-permute-done | bytes 1179680 | tf_op jit(solution)/shard_map/ppermute | solution.py:72
  409.3 25.8 %collective-permute-done.6 = bf16[256,2,1152]{2,0,1:T(8,128)(2,1)S(1)} collective-permute-done((bf16[256,2,1152]{2,0,1:T(8,128)(2,1)S(1)}, bf16[256,2,1152]{2,0,1:T(8,128)(2,1)S(1)}, u32[]{:S(2)}, u32[]{:S(2)}) %collective-permute-start.6) | collective-permute-done | bytes 1179680 | tf_op jit(solution)/shard_map/ppermute | solution.py:63
  444.6 11.3 %multiply_reduce_fusion = (f32[2,8,512]{2,1,0:T(8,128)S(1)}, f32[2,8,512,512]{2,3,1,0:T(8,128)}) fusion(f32[2,8,512,512]{2,3,1,0:T(8,128)} %get-tuple-element.63, f32[2,8,512]{2,1,0:T(8,128)S(1)} %log_add_fusion, bf16[2,512,8,72]{1,3,2,0:T(8,128)(2,1)S(1)} %bitcast.156, bf16[2,512,3,8,72]{1,4,3,2,0:T(8,128)(2,1)S(1)} %bitcast.150), kind=kOutput, calls=%fused_computation.1 | convolution fusion | flops 620748800 | bytes 35979264 | tf_op jit(solution)/shard_map/vmap(qhe,khe->hqk)/dot_general | solution.py:44
  455.9 12.2 %multiply_convert_fusion = bf16[2,8,512,512]{2,3,1,0:T(8,128)(2,1)S(1)} fusion(f32[2,8,512,512]{2,3,1,0:T(8,128)} %get-tuple-element.65, f32[2,8,512,512]{2,3,1,0:T(8,128)} %get-tuple-element.63, f32[2,8,512]{2,1,0:T(8,128)S(1)} %get-tuple-element.64, f32[2,8,512]{2,1,0:T(8,128)S(1)} %log_add_fusion), kind=kLoop, calls=%fused_computation | loop fusion | flops 20971520 | bytes 42008576 | tf_op jit(solution)/shard_map/vmap()/convert_element_type | solution.py:48
  480.1 24.9 %collective-permute-done.7 = bf16[256,2,1152]{2,0,1:T(8,128)(2,1)S(1)} collective-permute-done((bf16[256,2,1152]{2,0,1:T(8,128)(2,1)S(1)}, bf16[256,2,1152]{2,0,1:T(8,128)(2,1)S(1)}, u32[]{:S(2)}, u32[]{:S(2)}) %collective-permute-start.7) | collective-permute-done | bytes 1179680 | tf_op jit(solution)/shard_map/ppermute | solution.py:72
  518.9 11.4 %fusion.2 = bf16[2304,1152]{0,1:T(8,128)(2,1)} fusion(bf16[256,2,1152]{2,0,1:T(8,128)(2,1)} %collective-permute-done.4, bf16[256,2,1152]{2,0,1:T(8,128)(2,1)} %fusion.48, f32[512,2,2304]{2,0,1:T(8,128)} %fusion.21), kind=kOutput, calls=%fused_computation.12 | convolution fusion | flops 5464424448 | bytes 17104896 | tf_op jit(solution)/shard_map/sbf,sbd->fd/dot_general | solution.py:150
  549.7 18.4 %copy.128 = bf16[1152,3,576]{2,1,0:T(4,128)(2,1)} copy(bf16[1152,3,576]{2,0,1:T(8,128)(2,1)S(1)} %bitcast_convert_fusion) | data formatting | bytes 7962624
  568.1 12.3 %reshape.127 = bf16[1152,1728]{1,0:T(8,128)(2,1)} reshape(bf16[1152,3,576]{2,1,0:T(4,128)(2,1)} %copy.128) | data formatting | bytes 7962624
  592.1 20.1 %all_gather.27 = bf16[32,6,576]{2,1,0:T(8,128)(2,1)S(1)} all-gather(bf16[2,6,576]{2,1,0:T(8,128)(2,1)S(1)} %copy.102), channel_id=1, replica_groups=mesh['dp'=16,'tensor'=2] {'dp'}, dimensions={0}, use_global_device_ids=true | all-gather | bytes 235008 | tf_op jit(solution)/shard_map/all_gather | solution.py:205
  630.4 43.4 %reduce-scatter.15.cloned.1.call-done = bf16[2304,72]{0,1:T(8,128)(2,1)} async-done(((bf16[2304,1152]{0,1:T(8,128)(2,1)}), bf16[2304,72]{0,1:T(8,128)(2,1)}) %reduce-scatter.15.cloned.1.call-update) | async-done | bytes 331792 | tf_op jit(solution)/shard_map/reduce_scatter | solution.py:226
  675.7 81.3 %reduce-scatter.13.cloned.1.call-done = bf16[72,2304]{1,0:T(8,128)(2,1)} async-done(((bf16[1152,2304]{1,0:T(8,128)(2,1)}), bf16[72,2304]{1,0:T(8,128)(2,1)}) %reduce-scatter.13.cloned.1.call-update) | async-done | bytes 331792 | tf_op jit(solution)/shard_map/reduce_scatter | solution.py:223
  758.9 73.7 %reduce-scatter.19.cloned.1.call-done = bf16[72,1728]{1,0:T(8,128)(2,1)} async-done(((bf16[1152,1728]{1,0:T(8,128)(2,1)}), bf16[72,1728]{1,0:T(8,128)(2,1)}) %reduce-scatter.19.cloned.1.call-update) | async-done | bytes 248848
  (187 shorter events, 189.3 us)
Async XLA Ops:
  7.2 113.8 %all-reduce.4.cloned.1.call-start = ((), (), s32[]{:S(2)}) async-start(), calls=%async_computation.14 | async-start | bytes 983040
  31.4 89.6 %copy-start.20 = (bf16[32,1152]{1,0:T(8,128)(2,1)}, bf16[32,1152]{1,0:T(8,128)(2,1)S(1)}, u32[]{:S(2)}) copy-start(bf16[32,1152]{1,0:T(8,128)(2,1)S(1)} %reshape.109) | copy-start | bytes 221188
  32.5 142.7 %all-gather.6.cloned.1.call-start = ((), (), s32[]{:S(2)}) async-start(), calls=%async_computation.6 | async-start | bytes 4700160 | tf_op jit(solution)/shard_map/all_gather | solution.py:86
  33.3 180.8 %all-gather.8.cloned.1.call-start = ((), (), s32[]{:S(2)}) async-start(), calls=%async_computation.7 | async-start | bytes 1566720 | tf_op jit(solution)/shard_map/all_gather | solution.py:87
  34.0 250.6 %all-gather.10.cloned.1.call-start = ((), (), s32[]{:S(2)}) async-start(), calls=%async_computation.8 | async-start | bytes 5640192 | tf_op jit(solution)/shard_map/all_gather | solution.py:88
  34.6 293.7 %all-gather.12.cloned.1.call-start = ((), (), s32[]{:S(2)}) async-start(), calls=%async_computation.9 | async-start | bytes 5640192 | tf_op jit(solution)/shard_map/all_gather | solution.py:89
  36.1 111.4 %copy-start.21 = (f32[256,2]{0,1:T(2,128)}, f32[256,2]{0,1:T(2,128)S(1)}, u32[]{:S(2)}) copy-start(f32[256,2]{0,1:T(2,128)S(1)} %broadcast_multiply_fusion.5) | copy-start | bytes 6148
  36.6 111.0 %copy-start.23 = (f32[256,2]{0,1:T(2,128)}, f32[256,2]{0,1:T(2,128)S(1)}, u32[]{:S(2)}) copy-start(f32[256,2]{0,1:T(2,128)S(1)} %add_rsqrt_fusion.1) | copy-start | bytes 6148
  148.1 26.1 %collective-permute-start = (bf16[256,2,1152]{2,0,1:T(8,128)(2,1)S(1)}, bf16[256,2,1152]{2,0,1:T(8,128)(2,1)S(1)}, u32[]{:S(2)}, u32[]{:S(2)}) collective-permute-start(bf16[256,2,1152]{2,0,1:T(8,128)(2,1)S(1)} %fusion.41), channel_id=1, source_target_pairs={{0,1},{1,0},{2,3},{3,2},{4,5},{5,4},{6,7},{7,6},{8,9},{9,8},{10,11... | collective-permute-start | bytes 3538952 | tf_op jit(solution)/shard_map/ppermute | solution.py:63
  149.6 440.0 %reduce-scatter.17.cloned.1.call-start = ((), (), s32[]{:S(2)}) async-start(), calls=%async_computation.12 | async-start | bytes 884736
  221.4 28.3 %collective-permute-start.1 = (bf16[256,2,1152]{2,0,1:T(8,128)(2,1)}, bf16[256,2,1152]{2,0,1:T(8,128)(2,1)S(1)}, u32[]{:S(2)}, u32[]{:S(2)}) collective-permute-start(bf16[256,2,1152]{2,0,1:T(8,128)(2,1)} %slice.137), channel_id=1, source_target_pairs={{0,1},{1,0},{2,3},{3,2},{4,5},{5,4},{6,7},{7,6},{8,9},{9,8},{10,11... | collective-permute-start | bytes 3538952 | tf_op jit(solution)/shard_map/ppermute | solution.py:72
  255.4 29.2 %collective-permute-start.2 = (bf16[256,2,1152]{2,0,1:T(8,128)(2,1)}, bf16[256,2,1152]{2,0,1:T(8,128)(2,1)}, u32[]{:S(2)}, u32[]{:S(2)}) collective-permute-start(bf16[256,2,1152]{2,0,1:T(8,128)(2,1)} %add_convert_fusion.1), channel_id=1, source_target_pairs={{0,1},{1,0},{2,3},{3,2},{4,5},{5,4},{6,7},{7,6},{8,9},{9,8},{10,11... | collective-permute-start | bytes 3538952 | tf_op jit(solution)/shard_map/ppermute | solution.py:63
  261.0 47.5 %collective-permute-start.4 = (bf16[256,2,1152]{2,0,1:T(8,128)(2,1)}, bf16[256,2,1152]{2,0,1:T(8,128)(2,1)}, u32[]{:S(2)}, u32[]{:S(2)}) collective-permute-start(bf16[256,2,1152]{2,0,1:T(8,128)(2,1)} %fusion.48), channel_id=1, source_target_pairs={{0,1},{1,0},{2,3},{3,2},{4,5},{5,4},{6,7},{7,6},{8,9},{9,8},{10,11... | collective-permute-start | bytes 3538952 | tf_op jit(solution)/shard_map/ppermute | solution.py:63
  343.3 61.1 %slice-start = ((s8[4718592]{0:T(1024)(128)(4,1)}), s8[4194304]{0:T(1024)(128)(4,1)S(1)}, s32[]{:S(2)}) async-start(s8[4718592]{0:T(1024)(128)(4,1)} %bitcast.153), calls=%async_computation.16 | async-start | bytes 8388608
  350.8 53.6 %slice-start.1 = ((s8[4718592]{0:T(1024)(128)(4,1)}), s8[524288]{0:T(1024)(128)(4,1)S(1)}, s32[]{:S(2)}) async-start(s8[4718592]{0:T(1024)(128)(4,1)} %bitcast.153), calls=%async_computation.17 | async-start | bytes 1048576
  350.8 29.0 %collective-permute-start.5 = (bf16[256,2,1152]{2,0,1:T(8,128)(2,1)}, bf16[256,2,1152]{2,0,1:T(8,128)(2,1)S(1)}, u32[]{:S(2)}, u32[]{:S(2)}) collective-permute-start(bf16[256,2,1152]{2,0,1:T(8,128)(2,1)} %slice.135), channel_id=1, source_target_pairs={{0,1},{1,0},{2,3},{3,2},{4,5},{5,4},{6,7},{7,6},{8,9},{9,8},{10,11... | collective-permute-start | bytes 3538952 | tf_op jit(solution)/shard_map/ppermute | solution.py:72
  364.8 39.7 %collective-permute-start.3 = (bf16[256,2,1152]{2,0,1:T(8,128)(2,1)S(1)}, bf16[256,2,1152]{2,0,1:T(8,128)(2,1)S(1)}, u32[]{:S(2)}, u32[]{:S(2)}) collective-permute-start(bf16[256,2,1152]{2,0,1:T(8,128)(2,1)S(1)} %slice.136), channel_id=1, source_target_pairs={{0,1},{1,0},{2,3},{3,2},{4,5},{5,4},{6,7},{7,6},{8,9},{9,8},{10,11... | collective-permute-start | bytes 3538952 | tf_op jit(solution)/shard_map/ppermute | solution.py:72
  407.7 27.4 %collective-permute-start.6 = (bf16[256,2,1152]{2,0,1:T(8,128)(2,1)S(1)}, bf16[256,2,1152]{2,0,1:T(8,128)(2,1)S(1)}, u32[]{:S(2)}, u32[]{:S(2)}) collective-permute-start(bf16[256,2,1152]{2,0,1:T(8,128)(2,1)S(1)} %multiply_convert_fusion.4), channel_id=1, source_target_pairs={{0,1},{1,0},{2,3},{3,2},{4,5},{5,4},{6,7},{7,6},{8,9},{9,8},{10,11... | collective-permute-start | bytes 3538952 | tf_op jit(solution)/shard_map/ppermute | solution.py:63
  478.6 26.5 %collective-permute-start.7 = (bf16[256,2,1152]{2,0,1:T(8,128)(2,1)S(1)}, bf16[256,2,1152]{2,0,1:T(8,128)(2,1)S(1)}, u32[]{:S(2)}, u32[]{:S(2)}) collective-permute-start(bf16[256,2,1152]{2,0,1:T(8,128)(2,1)S(1)} %slice.134), channel_id=1, source_target_pairs={{0,1},{1,0},{2,3},{3,2},{4,5},{5,4},{6,7},{7,6},{8,9},{9,8},{10,11... | collective-permute-start | bytes 3538952 | tf_op jit(solution)/shard_map/ppermute | solution.py:72
  513.7 115.2 %reduce-scatter.21.cloned.1.call-start = ((), (), s32[]{:S(2)}) async-start(), calls=%async_computation.15 | async-start | bytes 1566720
  518.8 155.0 %reduce-scatter.15.cloned.1.call-start = ((), (), s32[]{:S(2)}) async-start(), calls=%async_computation.11 | async-start | bytes 5640192 | tf_op jit(solution)/shard_map/reduce_scatter | solution.py:226
  530.2 226.8 %reduce-scatter.13.cloned.1.call-start = ((), (), s32[]{:S(2)}) async-start(), calls=%async_computation.10 | async-start | bytes 5640192 | tf_op jit(solution)/shard_map/reduce_scatter | solution.py:223
  540.8 291.8 %reduce-scatter.19.cloned.1.call-start = ((), (), s32[]{:S(2)}) async-start(), calls=%async_computation.13 | async-start | bytes 4386816
  613.1 10.0 %all-to-all-start = ((f32[16,2,72]{2,1,0:T(2,128)}), f32[16,2,72]{2,1,0:T(2,128)S(1)}, u32[]{:S(2)}, u32[]{:S(2)}) async-start(f32[16,2,72]{2,1,0:T(2,128)} %bitcast.42), calls=%async_computation | async-start | bytes 32768 | tf_op jit(solution)/shard_map/all_to_all | solution.py:212
  (31 other events, 492.9 us)
Sparse Core Ops, SparseCore 0:
  32.6 88.3 all-reduce.3
  123.2 50.7 all-gather.5
  176.2 37.8 all-gather.7
  216.1 55.1 all-gather.9
  273.3 54.9 all-gather.11
  513.8 13.8 reduce-scatter.16
  531.9 58.7 reduce-scatter.20
  595.3 78.5 reduce-scatter.14
  678.4 78.5 reduce-scatter.12
  761.3 71.2 reduce-scatter.18

commit v2 on v1

v2 whole, which is shorter than its diff:
```python
import jax
import jax.numpy as jnp
from jax import lax
from jax.sharding import PartitionSpec as P

HEAD_DIM = 72


eps_norm = 1e-06


def layer_norm(values):
    centred = values - jnp.mean(values, axis=-1, keepdims=True)
    recip = lax.rsqrt(jnp.mean(centred * centred, axis=-1, keepdims=True) + eps_norm)
    return (centred * recip, recip)


def norm_back(grad_norm, normed, recip):
    inner = grad_norm - jnp.mean(grad_norm, axis=-1, keepdims=True)
    return recip * (inner - normed * jnp.mean(grad_norm * normed, axis=-1, keepdims=True))


def attend_one(queries, key_rows, value_rows):
    scores = jnp.einsum(
        "qhe,khe->hqk", queries, key_rows, preferred_element_type=jnp.float32
    ) * HEAD_DIM ** (-0.5)
    peak = jnp.max(scores, axis=-1, keepdims=True)
    raised = jnp.exp(scores - peak)
    total = jnp.sum(raised, axis=-1, keepdims=True)
    attn_probs = (raised / total).astype(jnp.bfloat16)
    attended = jnp.einsum(
        "hqk,khe->qhe", attn_probs, value_rows, preferred_element_type=jnp.float32
    )
    return (attended.astype(jnp.bfloat16), peak + jnp.log(total))


def attend_back(queries, key_rows, value_rows, grad_att, log_total):
    scale = HEAD_DIM ** (-0.5)
    scores = (
        jnp.einsum("qhe,khe->hqk", queries, key_rows, preferred_element_type=jnp.float32) * scale
    )
    attn_probs = jnp.exp(scores - log_total)
    probs_low = attn_probs.astype(jnp.bfloat16)
    grad_probs = jnp.einsum(
        "qhe,khe->hqk", grad_att, value_rows, preferred_element_type=jnp.float32
    )
    centre = jnp.sum(attn_probs * grad_probs, axis=-1, keepdims=True)
    grad_scores = (attn_probs * (grad_probs - centre)).astype(jnp.bfloat16)
    grad_q = (
        jnp.einsum("hqk,khe->qhe", grad_scores, key_rows, preferred_element_type=jnp.float32)
        * scale
    )
    grad_k = (
        jnp.einsum("hqk,qhe->khe", grad_scores, queries, preferred_element_type=jnp.float32) * scale
    )
    grad_v = jnp.einsum("hqk,qhe->khe", probs_low, grad_att, preferred_element_type=jnp.float32)
    return jnp.stack([grad_q, grad_k, grad_v], axis=1).astype(jnp.bfloat16)


SWAP = [(0, 1), (1, 0)]


def paired():
    return lax.axis_size("tensor") == 2


def spread(rows):
    if paired():
        return jnp.concatenate([rows, lax.ppermute(rows, "tensor", SWAP)], axis=0)
    return lax.all_gather(rows, "tensor", axis=0, tiled=True)


def shrink(terms, beside=()):
    terms = terms.astype(jnp.bfloat16)
    if paired():
        half = terms.shape[0] // 2
        other = lax.ppermute(terms[half:], "tensor", SWAP)
        other, beside = lax.optimization_barrier((other, beside))
        return terms[:half].astype(jnp.float32) + other.astype(jnp.float32), beside
    total = lax.psum_scatter(terms, "tensor", scatter_dimension=0, tiled=True)
    return total.astype(jnp.float32), beside


def widen(part):
    if paired():
        other = lax.ppermute(part, "tensor", SWAP)
        first = lax.axis_index("tensor") == 0
        return jnp.where(
            first,
            jnp.concatenate([part, other], axis=-1),
            jnp.concatenate([other, part], axis=-1),
        )
    return lax.all_gather(part, "tensor", axis=2, tiled=True)


def narrow(terms):
    if paired():
        half = terms.shape[2] // 2
        first = lax.axis_index("tensor") == 0
        low, high = terms[:, :, :half], terms[:, :, half:]
        other = lax.ppermute(jnp.where(first, high, low), "tensor", SWAP)
        return jnp.where(first, low, high) + other
    return lax.psum_scatter(terms, "tensor", scatter_dimension=2, tiled=True)


def scatter_rows(grad):
    return lax.psum_scatter(grad, "dp", scatter_dimension=0, tiled=True).astype(jnp.float32)


def body(latent_tokens, cond, mod_weight, qkv_weight, out_weight, fc1_weight, fc2_weight, grad_out):
    num_lat = latent_tokens.shape[1]
    local_dim = qkv_weight.shape[2]
    mod_rows = mod_weight.shape[0]
    cond_f = cond.astype(jnp.float32)
    silu_cond = jax.nn.silu(cond_f).astype(jnp.bfloat16)
    silu_rows = lax.all_to_all(silu_cond, "dp", split_axis=1, concat_axis=0, tiled=True)
    mod_terms = jnp.einsum(
        "bd,dke->bke", silu_rows, mod_weight, preferred_element_type=jnp.float32
    )
    mod_terms = mod_terms.reshape(-1, num_lat, 6 * local_dim)
    mod_terms = lax.all_to_all(mod_terms, "dp", split_axis=0, concat_axis=0, tiled=True)
    mod_part = jnp.sum(mod_terms, axis=0).reshape(num_lat, 6, local_dim)
    modulation = widen(mod_part)
    attn_rows = jnp.concatenate([qkv_weight.reshape(mod_rows, -1), out_weight.T], axis=1)
    attn_weight = lax.all_gather(attn_rows, "dp", axis=0, tiled=True)
    first_dense_weight = lax.all_gather(fc1_weight, "dp", axis=0, tiled=True)
    second_dense_weight = lax.all_gather(fc2_weight.T, "dp", axis=0, tiled=True)
    query_key_value_weight = attn_weight[:, : 3 * local_dim]
    output_projection_weight = attn_weight[:, 3 * local_dim :]
    local_heads = local_dim // HEAD_DIM
    shift_one, scale_one, gate_one, shift_two, scale_two, gate_two = [
        modulation[None, :, member] for member in range(6)
    ]
    block_inputs = latent_tokens.astype(jnp.float32)
    normed_one, recip_one = layer_norm(block_inputs)
    h_one = (normed_one * (1.0 + scale_one) + shift_one).astype(jnp.bfloat16)
    h_one_all = spread(h_one)
    seq_len = h_one_all.shape[0]
    triple = jnp.einsum(
        "sbd,de->sbe", h_one_all, query_key_value_weight, preferred_element_type=jnp.float32
    ).astype(jnp.bfloat16)
    by_latent = jnp.moveaxis(triple, 1, 0).reshape(num_lat, seq_len, 3, local_heads, HEAD_DIM)
    q_lat = by_latent[:, :, 0]
    k_lat = by_latent[:, :, 1]
    v_lat = by_latent[:, :, 2]
    att_lat, log_total = jax.vmap(attend_one)(q_lat, k_lat, v_lat)
    attended = jnp.moveaxis(att_lat, 0, 1).reshape(seq_len, num_lat, local_dim)
    rows = attended
    branch, _ = shrink(
        jnp.einsum(
            "sbh,dh->sbd", rows, output_projection_weight, preferred_element_type=jnp.float32
        )
    )
    middle = block_inputs + gate_one * branch
    normed_two, recip_two = layer_norm(middle)
    h_two = (normed_two * (1.0 + scale_two) + shift_two).astype(jnp.bfloat16)
    h_two_all = spread(h_two)
    hidden = jnp.einsum(
        "sbd,df->sbf", h_two_all, first_dense_weight, preferred_element_type=jnp.float32
    )
    active = jax.nn.gelu(hidden, approximate=True).astype(jnp.bfloat16)
    cotangent = grad_out.astype(jnp.float32)
    grad_mlp = (cotangent * gate_two).astype(jnp.bfloat16)
    grad_mlp_all = spread(grad_mlp)
    grad_fc2 = jnp.einsum(
        "sbd,sbf->df", grad_mlp_all, active, preferred_element_type=jnp.float32
    ).astype(jnp.bfloat16)
    second_dense_weight, grad_fc2 = lax.optimization_barrier((second_dense_weight, grad_fc2))
    grad_fc2 = scatter_rows(grad_fc2).T
    grad_active = jnp.einsum(
        "sbd,df->sbf", grad_mlp_all, second_dense_weight, preferred_element_type=jnp.float32
    )
    gelu_value, gelu_pull = jax.vjp(lambda inner: jax.nn.gelu(inner, approximate=True), hidden)
    grad_hidden = gelu_pull(grad_active)[0].astype(jnp.bfloat16)
    grad_fc1 = jnp.einsum(
        "sbd,sbf->df", h_two_all, grad_hidden, preferred_element_type=jnp.float32
    ).astype(jnp.bfloat16)
    grad_h_two, grad_fc1 = shrink(
        jnp.einsum(
            "sbf,df->sbd", grad_hidden, first_dense_weight, preferred_element_type=jnp.float32
        ),
        grad_fc1,
    )
    grad_fc1 = scatter_rows(grad_fc1)
    grad_shift_two = jnp.sum(grad_h_two, axis=0)
    grad_scale_two = jnp.sum(grad_h_two * normed_two, axis=0)
    grad_middle = cotangent + norm_back(grad_h_two * (1.0 + scale_two), normed_two, recip_two)
    grad_gate_one = jnp.sum(grad_middle * branch, axis=0)
    grad_branch = (grad_middle * gate_one).astype(jnp.bfloat16)
    mlp_terms = jnp.einsum(
        "sbf,df->sbd", active, second_dense_weight, preferred_element_type=jnp.float32
    ).astype(jnp.bfloat16)
    grad_branch_all, mlp_terms = lax.optimization_barrier((spread(grad_branch), mlp_terms))
    mlp_branch, _ = shrink(mlp_terms)
    out_block = (middle + gate_two * mlp_branch).astype(jnp.bfloat16)
    grad_gate_two = jnp.sum(cotangent * mlp_branch, axis=0)
    grad_wout = jnp.einsum(
        "sbd,sbh->dh", grad_branch_all, attended, preferred_element_type=jnp.float32
    )
    grad_att = jnp.einsum(
        "sbd,dh->sbh", grad_branch_all, output_projection_weight, preferred_element_type=jnp.float32
    ).astype(jnp.bfloat16)
    grad_att_lat = jnp.moveaxis(grad_att, 1, 0).reshape(num_lat, seq_len, local_heads, HEAD_DIM)
    grad_triple_lat = jax.vmap(attend_back)(q_lat, k_lat, v_lat, grad_att_lat, log_total)
    grad_triple = jnp.moveaxis(grad_triple_lat, 0, 1).reshape(seq_len, num_lat, 3 * local_dim)
    grad_wqkv = jnp.einsum("sbd,sbe->de", h_one_all, grad_triple, preferred_element_type=jnp.float32)
    grad_attn = jnp.concatenate([grad_wqkv, grad_wout], axis=1).astype(jnp.bfloat16)
    grad_h_one, grad_attn = shrink(
        jnp.einsum(
            "sbe,de->sbd", grad_triple, query_key_value_weight, preferred_element_type=jnp.float32
        ),
        grad_attn,
    )
    grad_attn = scatter_rows(grad_attn)
    grad_shift_one = jnp.sum(grad_h_one, axis=0)
    grad_scale_one = jnp.sum(grad_h_one * normed_one, axis=0)
    grad_input = grad_middle + norm_back(grad_h_one * (1.0 + scale_one), normed_one, recip_one)
    grad_mod_part = jnp.stack(
        [
            grad_shift_one,
            grad_scale_one,
            grad_gate_one,
            grad_shift_two,
            grad_scale_two,
            grad_gate_two,
        ],
        axis=1,
    )
    grad_mod = narrow(grad_mod_part).astype(jnp.bfloat16)
    grad_mod_all = lax.all_gather(grad_mod, "dp", axis=0, tiled=True)
    grad_wmod = jnp.einsum(
        "bd,bke->dke", silu_rows, grad_mod_all, preferred_element_type=jnp.float32
    )
    grad_silu_part = jnp.einsum(
        "bke,dke->bd", grad_mod_all, mod_weight, preferred_element_type=jnp.float32
    )
    grad_silu_part = lax.all_to_all(grad_silu_part, "dp", split_axis=0, concat_axis=1, tiled=True)
    if paired():
        grad_silu = grad_silu_part + lax.ppermute(grad_silu_part, "tensor", SWAP)
    else:
        grad_silu = lax.psum(grad_silu_part, "tensor")
    silu_value, silu_pull = jax.vjp(jax.nn.silu, cond_f)
    grad_condition = silu_pull(grad_silu)[0]
    grad_qkv = grad_attn[:, : 3 * local_dim].reshape(mod_rows, 3, local_dim)
    grad_out_weight = grad_attn[:, 3 * local_dim :].T
    return (
        out_block,
        grad_input,
        grad_condition,
        grad_wmod,
        grad_qkv,
        grad_out_weight,
        grad_fc1,
        grad_fc2,
    )


def solution(mesh):
    return jax.shard_map(
        body,
        mesh=mesh,
        in_specs=(
            P("tensor", "dp", None),
            P("dp", None),
            P("dp", None, "tensor"),
            P("dp", None, "tensor"),
            P("tensor", "dp"),
            P("dp", "tensor"),
            P("tensor", "dp"),
            P("tensor", "dp", None),
        ),
        out_specs=(
            P("tensor", "dp", None),
            P("tensor", "dp", None),
            P("dp", None),
            P("dp", None, "tensor"),
            P("dp", None, "tensor"),
            P("tensor", "dp"),
            P("dp", "tensor"),
            P("tensor", "dp"),
        ),
        check_vma=False,
    )
```

time: 850 us -> 476 us (0.56)
  waiting for transfers between devices: 486 us -> 169 us
  blocking collectives: 63.4 us -> 21.1 us
  local copies, waits for them, and re-layouts: 74.3 us -> 35.5 us
  other arithmetic: 45.6 us -> 58.9 us
  starting transfers between devices: 14.2 us -> 27.2 us
    unnamed x14 -> x7, waiting for transfers between devices: 160 us -> 0.78 us
    reduce_scatter x2, waiting for transfers between devices: 125 us -> 0.01 us  [scatter_rows(): lax.psum_scatter(grad, 'dp', scatter_dimension=0, tiled=True)]
    all_gather x2 -> x0, blocking collectives: 38.2 us -> none  [the longest x1 23.3 us: body(): silu_all = lax.all_gather(silu_cond, 'dp', axis=0, tiled=True)]
    unnamed x91 -> x123, local copies, waits for them, and re-layouts: 58.5 us -> 23.3 us
    all_gather x4 -> x3, waiting for transfers between devices: 25.9 us -> 0.01 us  [the longest x1 0.01 us: body(): attn_weight = lax.all_gather(attn_rows, 'dp', axis=0, tiled=True)]
    ppermute x8 -> x11, waiting for transfers between devices: 171 us -> 148 us  [the longest x4 74 us: spread(): return jnp.concatenate([rows, lax.ppermute(rows, 'tensor', SWAP)], axis=0)]
    all_to_all x0 -> x2, waiting for transfers between devices: none -> 19.8 us  [the longest x1 13.9 us: body(): lax.all_to_all(mod_terms, 'dp', split_axis=0, concat_axis=0, tiled=True)]
    slice x9 -> x5, local copies, waits for them, and re-layouts: 15.5 us -> 2.79 us  [the longest x4 2.73 us: shrink(): other = lax.ppermute(terms[half:], 'tensor', SWAP)]
  transfers between devices with their start and end apart: 19 -> 20, of which waited for: 15 -> 13; matrix products, arithmetic and copies ran while one was open for 21% -> 48% of each run, Pallas kernels for 0% -> 0%
where the time goes in v2:
time: 476 us; the launch traced here: 471 us
  waiting for transfers between devices  169 us (36%)
  matrix products  145 us (30%)
  other arithmetic  58.9 us (12%)
  local copies, waits for them, and re-layouts  35.5 us (7%)
  starting transfers between devices  27.2 us (6%)
  blocking collectives  21.1 us (4%)
  between operations  15.2 us (3%)
    ppermute x4, waiting for transfers between devices, spread(): return jnp.concatenate([rows, lax.ppermute(rows, 'tensor', SWAP)], axis=0)  74 us
    ppermute x4, waiting for transfers between devices, shrink(): other = lax.ppermute(terms[half:], 'tensor', SWAP)  68.9 us
    unnamed x123, local copies, waits for them, and re-layouts  23.3 us
    all_gather x1, blocking collectives, body(): grad_mod_all = lax.all_gather(grad_mod, 'dp', axis=0, tiled=True)  21.1 us
    dot_general x1, matrix products, body(): jnp.einsum('sbd,df->sbf', grad_mlp_all, second_dense_weight, preferred_el...  15.4 us
    all_to_all x1, waiting for transfers between devices, body(): lax.all_to_all(mod_terms, 'dp', split_axis=0, concat_axis=0, tiled=True)  13.9 us
    dot_general x1, matrix products, attend_back(): jnp.einsum('qhe,khe->hqk', grad_att, value_rows, preferred_element_type=j...  12.4 us
    convert_element_type x1, other arithmetic, attend_back(): grad_scores = (attn_probs * (grad_probs - centre)).astype(jnp.bfloat16)  12.3 us
  transfers between devices with their start and end apart: 20, of which 13 were waited for; matrix products, arithmetic and copies ran while one was open for 48% of the time, Pallas kernels for 0%

profile of v2, /device:TPU:0, one launch (start us, length us, event | category | flops | bytes accessed | tf_op | source)
XLA Modules:
  0.0 471.4 jit_solution(6469690396128149787)
XLA Ops:
  31.2 13.9 %all-to-all-done.1 = f32[16,2,3456]{2,1,0:T(2,128)S(1)} async-done(((f32[16,2,3456]{2,1,0:T(2,128)}), f32[16,2,3456]{2,1,0:T(2,128)S(1)}, u32[]{:S(2)}, u32[]{:S(2)}) %all-to-all-start.1) | async-done | bytes 442400 | tf_op jit(solution)/shard_map/all_to_all | solution.py:121
  52.4 25.6 %collective-permute-done.1 = bf16[256,2,1152]{2,0,1:T(8,128)(2,1)} collective-permute-done((bf16[256,2,1152]{2,0,1:T(8,128)(2,1)S(1)}, bf16[256,2,1152]{2,0,1:T(8,128)(2,1)}, u32[]{:S(2)}, u32[]{:S(2)}) %collective-permute-start.1) | collective-permute-done | bytes 1179680 | tf_op jit(solution)/shard_map/ppermute | solution.py:69
  78.1 7.7 %convolution_convert_fusion.2 = bf16[512,2,1728]{0,2,1:T(8,128)(2,1)S(1)} fusion(bf16[1152,2304]{1,0:T(8,128)(2,1)} %all-gather.4.cloned.1.call-done, bf16[256,2,1152]{2,0,1:T(8,128)(2,1)} %collective-permute-done.1, bf16[256,2,1152]{2,0,1:T(8,128)(2,1)} %copy-done.23), kind=kOutput, calls=%fused_computation.41 | convolution fusion | flops 4083351552 | bytes 10027008 | tf_op jit(solution)/shard_map/sbd,de->sbe/dot_general | solution.py:139
  92.9 8.6 %fusion = f32[2,8,512]{2,1,0:T(8,128)S(1)} fusion(f32[2,8,512,512]{2,3,1,0:T(8,128)} %get-tuple-element.77, f32[2,8,512]{2,1,0:T(8,128)S(1)} %get-tuple-element.76), kind=kLoop, calls=%fused_computation.5 | loop fusion | flops 12574720 | bytes 16842752 | tf_op jit(solution)/shard_map/vmap()/reduce_sum | solution.py:29
  101.6 8.4 %fusion.53 = bf16[2,8,72,512]{3,2,1,0:T(8,128)(2,1)S(1)} fusion(f32[2,8,512,512]{2,3,1,0:T(8,128)} %get-tuple-element.77, f32[2,8,512]{2,1,0:T(8,128)S(1)} %fusion, f32[2,8,512]{2,1,0:T(8,128)S(1)} %get-tuple-element.76, bf16[2,512,3,8,72]{1,4,3,2,0:T(8,128)(2,1)S(1)} %bitcast.142), kind=kOutput, calls=%fused_computation.91 | convolution fusion | flops 621346816 | bytes 19202048 | tf_op jit(solution)/shard_map/vmap(hqk,khe->qhe)/dot_general | solution.py:31
  116.5 24.9 %collective-permute-done.2 = bf16[256,2,1152]{2,0,1:T(8,128)(2,1)S(1)} collective-permute-done((bf16[256,2,1152]{2,0,1:T(8,128)(2,1)S(1)}, bf16[256,2,1152]{2,0,1:T(8,128)(2,1)S(1)}, u32[]{:S(2)}, u32[]{:S(2)}) %collective-permute-start.2) | collective-permute-done | bytes 1179680 | tf_op jit(solution)/shard_map/ppermute | solution.py:77
  148.9 24.7 %collective-permute-done.4 = bf16[256,2,1152]{2,0,1:T(8,128)(2,1)} collective-permute-done((bf16[256,2,1152]{2,0,1:T(8,128)(2,1)}, bf16[256,2,1152]{2,0,1:T(8,128)(2,1)}, u32[]{:S(2)}, u32[]{:S(2)}) %collective-permute-start.4) | collective-permute-done | bytes 1179680 | tf_op jit(solution)/shard_map/ppermute | solution.py:69
  173.6 9.5 %fusion.22 = f32[512,2,2304]{2,0,1:T(8,128)S(1)} fusion(bf16[1152,2304]{1,0:T(8,128)(2,1)} %all-gather.8.cloned.1.call-done, bf16[256,2,1152]{2,0,1:T(8,128)(2,1)} %collective-permute-done.4, bf16[256,2,1152]{2,0,1:T(8,128)(2,1)} %add_convert_fusion.1), kind=kOutput, calls=%fused_computation.34 | convolution fusion | flops 5440536576 | bytes 17104896 | tf_op jit(solution)/shard_map/sbd,df->sbf/dot_general | solution.py:158
  183.1 12.6 %collective-permute-done.3 = bf16[256,2,1152]{2,0,1:T(8,128)(2,1)} collective-permute-done((bf16[256,2,1152]{2,0,1:T(8,128)(2,1)}, bf16[256,2,1152]{2,0,1:T(8,128)(2,1)}, u32[]{:S(2)}, u32[]{:S(2)}) %collective-permute-start.3) | collective-permute-done | bytes 1179680 | tf_op jit(solution)/shard_map/ppermute | solution.py:69
  195.7 10.0 %fusion.1 = bf16[1152,2304]{1,0:T(8,128)(2,1)} fusion(bf16[256,2,1152]{2,0,1:T(8,128)(2,1)} %collective-permute-done.3, bf16[256,2,1152]{2,0,1:T(8,128)(2,1)} %fusion.45, f32[512,2,2304]{2,0,1:T(8,128)S(1)} %fusion.22), kind=kOutput, calls=%fused_computation.11 | convolution fusion | flops 5464424448 | bytes 17104896 | tf_op jit(solution)/shard_map/sbd,sbf->df/dot_general | solution.py:165
  205.8 15.4 %fusion.10 = bf16[512,2,2304]{2,0,1:T(8,128)(2,1)S(1)} fusion(f32[512,2,2304]{2,0,1:T(8,128)} %copy-done.53, bf16[1152,2304]{1,0:T(8,128)(2,1)} %all-gather.6.cloned.1.call-done, bf16[256,2,1152]{2,0,1:T(8,128)(2,1)} %collective-permute-done.3, bf16[256,2,1152]{2,0,1:T(8,128)(2,1)} %fusion.45), kind=kOutput, calls=%fused_computation.20 | convolution fusion | flops 5487722496 | bytes 21823488 | tf_op jit(solution)/shard_map/sbd,df->sbf/dot_general | solution.py:170
  221.2 9.4 %fusion.24 = bf16[512,2,1152]{2,0,1:T(8,128)(2,1)S(1)} fusion(bf16[512,2,2304]{2,0,1:T(8,128)(2,1)S(1)} %fusion.10, bf16[1152,2304]{1,0:T(8,128)(2,1)} %all-gather.8.cloned.1.call-done), kind=kOutput, calls=%fused_computation.37 | convolution fusion | flops 5436997632 | bytes 12386304 | tf_op jit(solution)/shard_map/sbf,df->sbd/dot_general | solution.py:179
  234.2 9.8 %fusion.2 = bf16[1152,2304]{1,0:T(8,128)(2,1)} fusion(bf16[512,2,2304]{2,0,1:T(8,128)(2,1)S(1)} %fusion.10, bf16[256,2,1152]{2,0,1:T(8,128)(2,1)} %collective-permute-done.4, bf16[256,2,1152]{2,0,1:T(8,128)(2,1)} %add_convert_fusion.1), kind=kOutput, calls=%fused_computation.12 | convolution fusion | flops 5443190784 | bytes 12386304 | tf_op jit(solution)/shard_map/sbd,sbf->df/dot_general | solution.py:175
  244.0 14.2 %collective-permute-done.5 = bf16[256,2,1152]{2,0,1:T(8,128)(2,1)} collective-permute-done((bf16[256,2,1152]{2,0,1:T(8,128)(2,1)}, bf16[256,2,1152]{2,0,1:T(8,128)(2,1)}, u32[]{:S(2)}, u32[]{:S(2)}) %collective-permute-start.5) | collective-permute-done | bytes 1179680 | tf_op jit(solution)/shard_map/ppermute | solution.py:77
  268.0 12.0 %fusion.27 = bf16[512,2,1152]{2,0,1:T(8,128)(2,1)} fusion(bf16[1152,2304]{1,0:T(8,128)(2,1)S(1)} %bitcast.162, f32[512,2,2304]{2,0,1:T(8,128)} %copy-done.53), kind=kOutput, calls=%fused_computation.38 | convolution fusion | flops 5458231296 | bytes 17104896 | tf_op jit(solution)/shard_map/sbf,df->sbd/dot_general | solution.py:190
  280.1 11.1 %collective-permute-done.6 = bf16[256,2,1152]{2,0,1:T(8,128)(2,1)} collective-permute-done((bf16[256,2,1152]{2,0,1:T(8,128)(2,1)S(1)}, bf16[256,2,1152]{2,0,1:T(8,128)(2,1)}, u32[]{:S(2)}, u32[]{:S(2)}) %collective-permute-start.6) | collective-permute-done | bytes 1179680 | tf_op jit(solution)/shard_map/ppermute | solution.py:69
  297.5 12.4 %multiply_reduce_fusion = (f32[2,8,512]{2,1,0:T(8,128)S(1)}, f32[2,8,512,512]{2,3,1,0:T(8,128)}) fusion(f32[2,8,512,512]{2,3,1,0:T(8,128)} %get-tuple-element.77, f32[2,8,512]{2,1,0:T(8,128)S(1)} %copy-done.25, bf16[2,512,8,72]{1,3,2,0:T(8,128)(2,1)S(1)} %bitcast.146, bf16[2,512,3,8,72]{1,4,3,2,0:T(8,128)(2,1)S(1)} %bitcast.143), kind=kOutput, calls=%fused_computation.1 | convolution fusion | flops 620748800 | bytes 35979264 | tf_op jit(solution)/shard_map/vmap(qhe,khe->hqk)/dot_general | solution.py:44
  309.9 12.3 %multiply_convert_fusion = bf16[2,8,512,512]{2,3,1,0:T(8,128)(2,1)S(1)} fusion(f32[2,8,512,512]{2,3,1,0:T(8,128)} %get-tuple-element.79, f32[2,8,512,512]{2,3,1,0:T(8,128)} %get-tuple-element.77, f32[2,8,512]{2,1,0:T(8,128)S(1)} %get-tuple-element.78, f32[2,8,512]{2,1,0:T(8,128)S(1)} %copy-done.25), kind=kLoop, calls=%fused_computation | loop fusion | flops 20971520 | bytes 42008576 | tf_op jit(solution)/shard_map/vmap()/convert_element_type | solution.py:48
  328.4 7.7 %fusion.59 = bf16[2,512,1,8,72]{1,4,3,0,2:T(8,128)(2,1)S(1)} fusion(bf16[2,512,8,72]{1,3,2,0:T(8,128)(2,1)S(1)} %bitcast.147, f32[2,8,512,512]{2,3,1,0:T(8,128)} %get-tuple-element.77, f32[2,8,512]{2,1,0:T(8,128)S(1)} %copy-done.25), kind=kOutput, calls=%fused_computation.97 | convolution fusion | flops 617152512 | bytes 19169280 | tf_op jit(solution)/shard_map/vmap(hqk,qhe->khe)/dot_general | solution.py:56
  336.9 7.5 %convolution_convert_fusion = bf16[512,2,1152]{2,0,1:T(8,128)(2,1)S(1)} fusion(bf16[512,2,1728]{0,2,1:T(8,128)(2,1)S(1)} %bitcast.148, bf16[1152,2304]{1,0:T(8,128)(2,1)} %all-gather.4.cloned.1.call-done), kind=kOutput, calls=%fused_computation.39 | convolution fusion | flops 4078043136 | bytes 10027008 | tf_op jit(solution)/shard_map/sbe,de->sbd/dot_general | solution.py:209
  357.4 10.5 %collective-permute-done.8 = bf16[256,2,1152]{2,0,1:T(8,128)(2,1)} collective-permute-done((bf16[256,2,1152]{2,0,1:T(8,128)(2,1)S(1)}, bf16[256,2,1152]{2,0,1:T(8,128)(2,1)}, u32[]{:S(2)}, u32[]{:S(2)}) %collective-permute-start.8) | collective-permute-done | bytes 1179680 | tf_op jit(solution)/shard_map/ppermute | solution.py:77
  367.9 8.6 %copy.114 = bf16[1152,2304]{1,0:T(8,128)(2,1)} copy(bf16[1152,2304]{0,1:T(8,128)(2,1)} %pad_maximum_fusion) | data formatting | bytes 10616832
  381.0 19.3 %collective-permute-done.7 = bf16[256,2,1152]{2,0,1:T(8,128)(2,1)S(1)} collective-permute-done((bf16[256,2,1152]{2,0,1:T(8,128)(2,1)S(1)}, bf16[256,2,1152]{2,0,1:T(8,128)(2,1)S(1)}, u32[]{:S(2)}, u32[]{:S(2)}) %collective-permute-start.7) | collective-permute-done | bytes 1179680 | tf_op jit(solution)/shard_map/ppermute | solution.py:77
  416.1 21.1 %all_gather.15 = bf16[32,6,576]{2,1,0:T(8,128)(2,1)S(1)} all-gather(bf16[2,6,576]{2,1,0:T(8,128)(2,1)S(1)} %add_convert_fusion.2), channel_id=1, replica_groups=mesh['dp'=16,'tensor'=2] {'dp'}, dimensions={0}, use_global_device_ids=true | all-gather | bytes 235008 | tf_op jit(solution)/shard_map/all_gather | solution.py:230
  (231 shorter events, 139.0 us)
Async XLA Ops:
  7.2 70.9 %all-gather.4.cloned.1.call-start = ((), (), s32[]{:S(2)}) async-start(), calls=%async_computation.6 | async-start | bytes 5640192 | tf_op jit(solution)/shard_map/all_gather | solution.py:125
  10.4 138.5 %all-gather.8.cloned.1.call-start = ((), (), s32[]{:S(2)}) async-start(), calls=%async_computation.8 | async-start | bytes 5640192 | tf_op jit(solution)/shard_map/all_gather | solution.py:126
  11.9 13.8 %all-to-all-start = ((bf16[2,16,72]{2,0,1:T(2,128)(2,1)}), bf16[2,16,72]{2,0,1:T(2,128)(2,1)S(1)}, u32[]{:S(2)}, u32[]{:S(2)}) async-start(bf16[2,16,72]{2,0,1:T(2,128)(2,1)} %copy.82), calls=%async_computation | async-start | bytes 16384 | tf_op jit(solution)/shard_map/all_to_all | solution.py:116
  26.9 18.2 %all-to-all-start.1 = ((f32[16,2,3456]{2,1,0:T(2,128)}), f32[16,2,3456]{2,1,0:T(2,128)S(1)}, u32[]{:S(2)}, u32[]{:S(2)}) async-start(f32[16,2,3456]{2,1,0:T(2,128)} %copy.85), calls=%async_computation.1 | async-start | bytes 884736 | tf_op jit(solution)/shard_map/all_to_all | solution.py:121
  30.5 175.2 %all-gather.6.cloned.1.call-start = ((), (), s32[]{:S(2)}) async-start(), calls=%async_computation.7 | async-start | bytes 5640192 | tf_op jit(solution)/shard_map/all_gather | solution.py:127
  45.4 4.0 collective-permute-start
  46.8 38.9 %copy-start.46 = (f32[256,2]{0,1:T(2,128)}, f32[256,2]{0,1:T(2,128)S(1)}, u32[]{:S(2)}) copy-start(f32[256,2]{0,1:T(2,128)S(1)} %add_rsqrt_fusion.1) | copy-start | bytes 6148
  50.1 27.9 %copy-start.28 = (f32[2,1152]{1,0:T(2,128)}, f32[2,1152]{1,0:T(2,128)S(1)}, u32[]{:S(2)}) copy-start(f32[2,1152]{1,0:T(2,128)S(1)} %get-tuple-element.83) | copy-start | bytes 27652
  50.7 27.4 %collective-permute-start.1 = (bf16[256,2,1152]{2,0,1:T(8,128)(2,1)S(1)}, bf16[256,2,1152]{2,0,1:T(8,128)(2,1)}, u32[]{:S(2)}, u32[]{:S(2)}) collective-permute-start(bf16[256,2,1152]{2,0,1:T(8,128)(2,1)S(1)} %fusion.38), channel_id=1, source_target_pairs={{0,1},{1,0},{2,3},{3,2},{4,5},{5,4},{6,7},{7,6},{8,9},{9,8},{10,11... | collective-permute-start | bytes 3538952 | tf_op jit(solution)/shard_map/ppermute | solution.py:69
  52.2 405.0 %reduce-scatter.8.cloned.1.call-start = ((), (), s32[]{:S(2)}) async-start(), calls=%async_computation.10 | async-start | bytes 5640192 | tf_op jit(solution)/shard_map/reduce_scatter | solution.py:107
  114.5 27.4 %copy-start.10 = (bf16[512,2,1152]{2,0,1:T(8,128)(2,1)}, bf16[512,2,1152]{2,0,1:T(8,128)(2,1)S(1)}, u32[]{:S(2)}) copy-start(bf16[512,2,1152]{2,0,1:T(8,128)(2,1)S(1)} %convolution_convert_fusion.1) | copy-start | bytes 7077892
  114.6 26.7 %collective-permute-start.2 = (bf16[256,2,1152]{2,0,1:T(8,128)(2,1)S(1)}, bf16[256,2,1152]{2,0,1:T(8,128)(2,1)S(1)}, u32[]{:S(2)}, u32[]{:S(2)}) collective-permute-start(bf16[256,2,1152]{2,0,1:T(8,128)(2,1)S(1)} %slice.101), channel_id=1, source_target_pairs={{0,1},{1,0},{2,3},{3,2},{4,5},{5,4},{6,7},{7,6},{8,9},{9,8},{10,11... | collective-permute-start | bytes 3538952 | tf_op jit(solution)/shard_map/ppermute | solution.py:77
  144.3 29.2 %collective-permute-start.4 = (bf16[256,2,1152]{2,0,1:T(8,128)(2,1)}, bf16[256,2,1152]{2,0,1:T(8,128)(2,1)}, u32[]{:S(2)}, u32[]{:S(2)}) collective-permute-start(bf16[256,2,1152]{2,0,1:T(8,128)(2,1)} %add_convert_fusion.1), channel_id=1, source_target_pairs={{0,1},{1,0},{2,3},{3,2},{4,5},{5,4},{6,7},{7,6},{8,9},{9,8},{10,11... | collective-permute-start | bytes 3538952 | tf_op jit(solution)/shard_map/ppermute | solution.py:69
  147.7 48.0 %collective-permute-start.3 = (bf16[256,2,1152]{2,0,1:T(8,128)(2,1)}, bf16[256,2,1152]{2,0,1:T(8,128)(2,1)}, u32[]{:S(2)}, u32[]{:S(2)}) collective-permute-start(bf16[256,2,1152]{2,0,1:T(8,128)(2,1)} %fusion.45), channel_id=1, source_target_pairs={{0,1},{1,0},{2,3},{3,2},{4,5},{5,4},{6,7},{7,6},{8,9},{9,8},{10,11... | collective-permute-start | bytes 3538952 | tf_op jit(solution)/shard_map/ppermute | solution.py:69
  205.7 253.3 %reduce-scatter.6.cloned.1.call-start = ((), (), s32[]{:S(2)}) async-start(), calls=%async_computation.9 | async-start | bytes 5640192 | tf_op jit(solution)/shard_map/reduce_scatter | solution.py:107
  233.0 25.2 %collective-permute-start.5 = (bf16[256,2,1152]{2,0,1:T(8,128)(2,1)}, bf16[256,2,1152]{2,0,1:T(8,128)(2,1)}, u32[]{:S(2)}, u32[]{:S(2)}) collective-permute-start(bf16[256,2,1152]{2,0,1:T(8,128)(2,1)} %slice.106), channel_id=1, source_target_pairs={{0,1},{1,0},{2,3},{3,2},{4,5},{5,4},{6,7},{7,6},{8,9},{9,8},{10,11... | collective-permute-start | bytes 3538952 | tf_op jit(solution)/shard_map/ppermute | solution.py:77
  267.1 24.1 %collective-permute-start.6 = (bf16[256,2,1152]{2,0,1:T(8,128)(2,1)S(1)}, bf16[256,2,1152]{2,0,1:T(8,128)(2,1)}, u32[]{:S(2)}, u32[]{:S(2)}) collective-permute-start(bf16[256,2,1152]{2,0,1:T(8,128)(2,1)S(1)} %multiply_convert_fusion.4), channel_id=1, source_target_pairs={{0,1},{1,0},{2,3},{3,2},{4,5},{5,4},{6,7},{7,6},{8,9},{9,8},{10,11... | collective-permute-start | bytes 3538952 | tf_op jit(solution)/shard_map/ppermute | solution.py:69
  280.0 180.9 %reduce-scatter.10.cloned.1.call-start = ((), (), s32[]{:S(2)}) async-start(), calls=%async_computation.11 | async-start | bytes 5640192
  344.5 23.3 %collective-permute-start.8 = (bf16[256,2,1152]{2,0,1:T(8,128)(2,1)S(1)}, bf16[256,2,1152]{2,0,1:T(8,128)(2,1)}, u32[]{:S(2)}, u32[]{:S(2)}) collective-permute-start(bf16[256,2,1152]{2,0,1:T(8,128)(2,1)S(1)} %slice.108), channel_id=1, source_target_pairs={{0,1},{1,0},{2,3},{3,2},{4,5},{5,4},{6,7},{7,6},{8,9},{9,8},{10,11... | collective-permute-start | bytes 3538952 | tf_op jit(solution)/shard_map/ppermute | solution.py:77
  378.0 22.3 %collective-permute-start.7 = (bf16[256,2,1152]{2,0,1:T(8,128)(2,1)S(1)}, bf16[256,2,1152]{2,0,1:T(8,128)(2,1)S(1)}, u32[]{:S(2)}, u32[]{:S(2)}) collective-permute-start(bf16[256,2,1152]{2,0,1:T(8,128)(2,1)S(1)} %slice.85), channel_id=1, source_target_pairs={{0,1},{1,0},{2,3},{3,2},{4,5},{5,4},{6,7},{7,6},{8,9},{9,8},{10,11... | collective-permute-start | bytes 3538952 | tf_op jit(solution)/shard_map/ppermute | solution.py:77
  403.9 40.1 %copy-start.3 = (f32[256,2,1152]{2,0,1:T(8,128)S(1)}, f32[256,2,1152]{2,0,1:T(8,128)}, u32[]{:S(2)}) copy-start(f32[256,2,1152]{2,0,1:T(8,128)} %copy-done.2) | copy-start | bytes 7077892
  411.1 4.1 collective-permute-start.9
  439.9 12.1 %all-to-all-start.2 = ((f32[16,2,72]{2,1,0:T(2,128)}), f32[16,2,72]{2,1,0:T(2,128)}, u32[]{:S(2)}, u32[]{:S(2)}) async-start(f32[16,2,72]{2,1,0:T(2,128)} %bitcast.158), calls=%async_computation.2 | async-start | bytes 32768 | tf_op jit(solution)/shard_map/all_to_all | solution.py:237
  452.8 3.7 collective-permute-start.10
  (52 other events, 517.9 us)
Sparse Core Ops, SparseCore 0:
  10.8 62.4 all-gather.3
  75.5 54.9 all-gather.7
  132.6 54.9 all-gather.5
  205.9 79.3 reduce-scatter.7
  289.1 78.7 reduce-scatter.5
  376.6 80.4 reduce-scatter.9

commit v3 on v2

--- a/solution.py
+++ b/solution.py
@@ -70,6 +70,18 @@
     return lax.all_gather(rows, "tensor", axis=0, tiled=True)
 
 
+def fetch(rows):
+    if paired():
+        return lax.ppermute(rows, "tensor", SWAP)
+    return lax.all_gather(rows, "tensor", axis=0, tiled=True)
+
+
+def over_all(rows, fetched, change):
+    if paired():
+        return jnp.concatenate([change(rows), change(fetched)], axis=0)
+    return change(fetched)
+
+
 def shrink(terms, beside=()):
     terms = terms.astype(jnp.bfloat16)
     if paired():
@@ -119,22 +131,28 @@
     )
     mod_terms = mod_terms.reshape(-1, num_lat, 6 * local_dim)
     mod_terms = lax.all_to_all(mod_terms, "dp", split_axis=0, concat_axis=0, tiled=True)
+    mod_terms, latent_fetched = lax.optimization_barrier((mod_terms, fetch(latent_tokens)))
     mod_part = jnp.sum(mod_terms, axis=0).reshape(num_lat, 6, local_dim)
     modulation = widen(mod_part)
-    attn_rows = jnp.concatenate([qkv_weight.reshape(mod_rows, -1), out_weight.T], axis=1)
-    attn_weight = lax.all_gather(attn_rows, "dp", axis=0, tiled=True)
+    query_key_value_weight = lax.all_gather(
+        qkv_weight.reshape(mod_rows, -1), "dp", axis=0, tiled=True
+    )
+    output_projection_weight = lax.all_gather(out_weight.T, "dp", axis=0, tiled=True)
     first_dense_weight = lax.all_gather(fc1_weight, "dp", axis=0, tiled=True)
     second_dense_weight = lax.all_gather(fc2_weight.T, "dp", axis=0, tiled=True)
-    query_key_value_weight = attn_weight[:, : 3 * local_dim]
-    output_projection_weight = attn_weight[:, 3 * local_dim :]
     local_heads = local_dim // HEAD_DIM
     shift_one, scale_one, gate_one, shift_two, scale_two, gate_two = [
         modulation[None, :, member] for member in range(6)
     ]
     block_inputs = latent_tokens.astype(jnp.float32)
     normed_one, recip_one = layer_norm(block_inputs)
-    h_one = (normed_one * (1.0 + scale_one) + shift_one).astype(jnp.bfloat16)
-    h_one_all = spread(h_one)
+    h_one_all = over_all(
+        latent_tokens,
+        latent_fetched,
+        lambda rows: (
+            layer_norm(rows.astype(jnp.float32))[0] * (1.0 + scale_one) + shift_one
+        ).astype(jnp.bfloat16),
+    )
     seq_len = h_one_all.shape[0]
     triple = jnp.einsum(
         "sbd,de->sbe", h_one_all, query_key_value_weight, preferred_element_type=jnp.float32
@@ -145,6 +163,7 @@
     v_lat = by_latent[:, :, 2]
     att_lat, log_total = jax.vmap(attend_one)(q_lat, k_lat, v_lat)
     attended = jnp.moveaxis(att_lat, 0, 1).reshape(seq_len, num_lat, local_dim)
+    attended, grad_out_fetched = lax.optimization_barrier((attended, fetch(grad_out)))
     rows = attended
     branch, _ = shrink(
         jnp.einsum(
@@ -160,8 +179,11 @@
     )
     active = jax.nn.gelu(hidden, approximate=True).astype(jnp.bfloat16)
     cotangent = grad_out.astype(jnp.float32)
-    grad_mlp = (cotangent * gate_two).astype(jnp.bfloat16)
-    grad_mlp_all = spread(grad_mlp)
+    grad_mlp_all = over_all(
+        grad_out,
+        grad_out_fetched,
+        lambda rows: (rows.astype(jnp.float32) * gate_two).astype(jnp.bfloat16),
+    )
     grad_fc2 = jnp.einsum(
         "sbd,sbf->df", grad_mlp_all, active, preferred_element_type=jnp.float32
     ).astype(jnp.bfloat16)
@@ -191,17 +213,17 @@
         "sbf,df->sbd", active, second_dense_weight, preferred_element_type=jnp.float32
     ).astype(jnp.bfloat16)
     grad_branch_all, mlp_terms = lax.optimization_barrier((spread(grad_branch), mlp_terms))
-    mlp_branch, _ = shrink(mlp_terms)
+    grad_wout = jnp.einsum(
+        "sbd,sbh->dh", grad_branch_all, attended, preferred_element_type=jnp.float32
+    )
+    grad_att = jnp.einsum(
+        "sbd,dh->sbh", grad_branch_all, output_projection_weight, preferred_element_type=jnp.float32
+    ).astype(jnp.bfloat16)
+    grad_att_lat = jnp.moveaxis(grad_att, 1, 0).reshape(num_lat, seq_len, local_heads, HEAD_DIM)
+    grad_triple_lat = jax.vmap(attend_back)(q_lat, k_lat, v_lat, grad_att_lat, log_total)
+    mlp_branch, grad_triple_lat = shrink(mlp_terms, grad_triple_lat)
     out_block = (middle + gate_two * mlp_branch).astype(jnp.bfloat16)
     grad_gate_two = jnp.sum(cotangent * mlp_branch, axis=0)
-    grad_wout = jnp.einsum(
-        "sbd,sbh->dh", grad_branch_all, attended, preferred_element_type=jnp.float32
-    )
-    grad_att = jnp.einsum(
-        "sbd,dh->sbh", grad_branch_all, output_projection_weight, preferred_element_type=jnp.float32
-    ).astype(jnp.bfloat16)
-    grad_att_lat = jnp.moveaxis(grad_att, 1, 0).reshape(num_lat, seq_len, local_heads, HEAD_DIM)
-    grad_triple_lat = jax.vmap(attend_back)(q_lat, k_lat, v_lat, grad_att_lat, log_total)
     grad_triple = jnp.moveaxis(grad_triple_lat, 0, 1).reshape(seq_len, num_lat, 3 * local_dim)
     grad_wqkv = jnp.einsum("sbd,sbe->de", h_one_all, grad_triple, preferred_element_type=jnp.float32)
     grad_attn = jnp.concatenate([grad_wqkv, grad_wout], axis=1).astype(jnp.bfloat16)

time: 476 us -> 509 us (1.069)
  local copies, waits for them, and re-layouts: 35.5 us -> 51.8 us
  waiting for transfers between devices: 169 us -> 183 us
  matrix products: 145 us -> 137 us
    ppermute x4 -> x2, waiting for transfers between devices: 74 us -> 36.4 us  [spread(): return jnp.concatenate([rows, lax.ppermute(rows, 'tensor', SWAP)], axis=0)]
    all_gather x1, waiting for transfers between devices: 0.01 us -> 31.3 us  [body(): second_dense_weight = lax.all_gather(fc2_weight.T, 'dp', axis=0, tiled=True)]
    unnamed x7 -> x8, waiting for transfers between devices: 0.78 us -> 15.3 us
    ppermute x1, waiting for transfers between devices: 2.52 us -> 15.6 us  [widen(): other = lax.ppermute(part, 'tensor', SWAP)]
    unnamed x123 -> x138, local copies, waits for them, and re-layouts: 23.3 us -> 34.5 us
    ppermute x4, waiting for transfers between devices: 68.9 us -> 62.5 us  [shrink(): other = lax.ppermute(terms[half:], 'tensor', SWAP)]
  transfers between devices with their start and end apart: 20 -> 21, of which waited for: 13 -> 14; matrix products, arithmetic and copies ran while one was open for 48% -> 46% of each run, Pallas kernels for 0% -> 0%
where the time goes in v3:
time: 509 us; the launch traced here: 500 us
  waiting for transfers between devices  183 us (36%)
  matrix products  137 us (27%)
  other arithmetic  62.7 us (12%)
  local copies, waits for them, and re-layouts  51.8 us (10%)
  starting transfers between devices  29.5 us (6%)
  blocking collectives  20.5 us (4%)
  between operations  15.1 us (3%)
    ppermute x4, waiting for transfers between devices, shrink(): other = lax.ppermute(terms[half:], 'tensor', SWAP)  62.5 us
    ppermute x2, waiting for transfers between devices, spread(): return jnp.concatenate([rows, lax.ppermute(rows, 'tensor', SWAP)], axis=0)  36.4 us
    unnamed x138, local copies, waits for them, and re-layouts  34.5 us
    all_gather x1, waiting for transfers between devices, body(): second_dense_weight = lax.all_gather(fc2_weight.T, 'dp', axis=0, tiled=True)  31.3 us
    all_gather x1, blocking collectives, body(): grad_mod_all = lax.all_gather(grad_mod, 'dp', axis=0, tiled=True)  20.5 us
    ppermute x1, waiting for transfers between devices, widen(): other = lax.ppermute(part, 'tensor', SWAP)  15.6 us
    unnamed x8, waiting for transfers between devices  15.3 us
    dot_general x1, matrix products, body(): jnp.einsum('sbd,df->sbf', grad_mlp_all, second_dense_weight, preferred_el...  15.1 us
  transfers between devices with their start and end apart: 21, of which 14 were waited for; matrix products, arithmetic and copies ran while one was open for 46% of the time, Pallas kernels for 0%

profile of v3, /device:TPU:0, one launch (start us, length us, event | category | flops | bytes accessed | tf_op | source)
XLA Modules:
  0.0 499.7 jit_solution(15696368393287349933)
XLA Ops:
  34.9 14.4 %all-to-all-done.1 = f32[16,2,3456]{2,1,0:T(2,128)S(1)} async-done(((f32[16,2,3456]{2,1,0:T(2,128)}), f32[16,2,3456]{2,1,0:T(2,128)S(1)}, u32[]{:S(2)}, u32[]{:S(2)}) %all-to-all-start.1) | async-done | bytes 442400 | tf_op jit(solution)/shard_map/all_to_all | solution.py:133
  51.8 15.6 %collective-permute-done.1 = f32[2,6,576]{2,1,0:T(8,128)S(1)} collective-permute-done((f32[2,6,576]{2,1,0:T(8,128)S(1)}, f32[2,6,576]{2,1,0:T(8,128)S(1)}, u32[]{:S(2)}, u32[]{:S(2)}) %collective-permute-start.1) | collective-permute-done | bytes 27680 | tf_op jit(solution)/shard_map/ppermute | solution.py:98
  72.0 7.8 %fusion.37 = bf16[512,2,1728]{0,2,1:T(8,128)(2,1)S(1)} fusion(bf16[1152,1728]{1,0:T(8,128)(2,1)} %all-gather.5.cloned.1.call-done, bf16[256,2,1152]{2,0,1:T(8,128)(2,1)} %get-tuple-element.89, bf16[256,2,1152]{2,0,1:T(8,128)(2,1)S(1)} %get-tuple-element.88), kind=kOutput, calls=%fused_computation.44 | convolution fusion | flops 4083351552 | bytes 9879552 | tf_op jit(solution)/shard_map/sbd,de->sbe/dot_general | solution.py:157
  79.8 7.6 %multiply_reduce_fusion.1 = (f32[2,8,512]{2,1,0:T(8,128)S(1)}, f32[2,8,512,512]{2,3,1,0:T(8,128)}) fusion(bf16[2,512,3,8,72]{1,4,3,2,0:T(8,128)(2,1)S(1)} %bitcast.145), kind=kOutput, calls=%fused_computation.6 | convolution fusion | flops 612360192 | bytes 19169280 | tf_op jit(solution)/shard_map/vmap(qhe,khe->hqk)/dot_general | solution.py:24
  87.4 8.8 %fusion = f32[2,8,512]{2,1,0:T(8,128)S(1)} fusion(f32[2,8,512,512]{2,3,1,0:T(8,128)} %get-tuple-element.93, f32[2,8,512]{2,1,0:T(8,128)S(1)} %get-tuple-element.92), kind=kLoop, calls=%fused_computation.5 | loop fusion | flops 12574720 | bytes 16842752 | tf_op jit(solution)/shard_map/vmap()/reduce_sum | solution.py:29
  96.2 8.1 %fusion.69 = bf16[2,8,72,512]{3,2,1,0:T(8,128)(2,1)S(1)} fusion(f32[2,8,512,512]{2,3,1,0:T(8,128)} %get-tuple-element.93, f32[2,8,512]{2,1,0:T(8,128)S(1)} %fusion, f32[2,8,512]{2,1,0:T(8,128)S(1)} %get-tuple-element.92, bf16[2,512,3,8,72]{1,4,3,2,0:T(8,128)(2,1)} %bitcast.146), kind=kOutput, calls=%fused_computation.103 | convolution fusion | flops 621346816 | bytes 19202048 | tf_op jit(solution)/shard_map/vmap(hqk,khe->qhe)/dot_general | solution.py:31
  111.9 26.6 %collective-permute-done.3 = bf16[256,2,1152]{2,0,1:T(8,128)(2,1)S(1)} collective-permute-done((bf16[256,2,1152]{2,0,1:T(8,128)(2,1)S(1)}, bf16[256,2,1152]{2,0,1:T(8,128)(2,1)S(1)}, u32[]{:S(2)}, u32[]{:S(2)}) %collective-permute-start.3) | collective-permute-done | bytes 1179680 | tf_op jit(solution)/shard_map/ppermute | solution.py:89
  145.9 22.1 %collective-permute-done.4 = bf16[256,2,1152]{2,0,1:T(8,128)(2,1)} collective-permute-done((bf16[256,2,1152]{2,0,1:T(8,128)(2,1)S(1)}, bf16[256,2,1152]{2,0,1:T(8,128)(2,1)}, u32[]{:S(2)}, u32[]{:S(2)}) %collective-permute-start.4) | collective-permute-done | bytes 1179680 | tf_op jit(solution)/shard_map/ppermute | solution.py:69
  168.0 9.6 %fusion.22 = f32[512,2,2304]{2,0,1:T(8,128)S(1)} fusion(bf16[1152,2304]{1,0:T(8,128)(2,1)} %all-gather.11.cloned.1.call-done, bf16[256,2,1152]{2,0,1:T(8,128)(2,1)} %collective-permute-done.4, bf16[256,2,1152]{2,0,1:T(8,128)(2,1)} %copy-done.26), kind=kOutput, calls=%fused_computation.34 | convolution fusion | flops 5440536576 | bytes 17104896 | tf_op jit(solution)/shard_map/sbd,df->sbf/dot_general | solution.py:177
  181.2 8.4 %fusion.1 = bf16[1152,2304]{1,0:T(8,128)(2,1)} fusion(bf16[256,2,1152]{2,0,1:T(8,128)(2,1)S(1)} %copy-done.29, bf16[256,2,1152]{2,0,1:T(8,128)(2,1)S(1)} %copy-done.28, f32[512,2,2304]{2,0,1:T(8,128)S(1)} %fusion.22), kind=kOutput, calls=%fused_computation.11 | convolution fusion | flops 5464424448 | bytes 17104896 | tf_op jit(solution)/shard_map/sbd,sbf->df/dot_general | solution.py:187
  189.7 31.3 %all-gather.9.cloned.1.call-done = bf16[1152,2304]{1,0:T(8,128)(2,1)} async-done(((bf16[72,2304]{1,0:T(8,128)(2,1)}), bf16[1152,2304]{1,0:T(8,128)(2,1)}) %all-gather.9.cloned.1.call-update) | async-done | bytes 5308432 | tf_op jit(solution)/shard_map/all_gather | solution.py:142
  221.0 15.1 %fusion.10 = bf16[512,2,2304]{2,0,1:T(8,128)(2,1)S(1)} fusion(f32[512,2,2304]{2,0,1:T(8,128)} %copy-done.59, bf16[1152,2304]{1,0:T(8,128)(2,1)} %all-gather.9.cloned.1.call-done, bf16[256,2,1152]{2,0,1:T(8,128)(2,1)} %get-tuple-element.91, bf16[256,2,1152]{2,0,1:T(8,128)(2,1)} %get-tuple-element.90), kind=kOutput, calls=%fused_computation.20 | convolution fusion | flops 5487722496 | bytes 21823488 | tf_op jit(solution)/shard_map/sbd,df->sbf/dot_general | solution.py:192
  236.1 9.5 %fusion.28 = bf16[512,2,1152]{2,0,1:T(8,128)(2,1)S(1)} fusion(bf16[512,2,2304]{2,0,1:T(8,128)(2,1)S(1)} %fusion.10, bf16[1152,2304]{1,0:T(8,128)(2,1)} %all-gather.11.cloned.1.call-done), kind=kOutput, calls=%fused_computation.40 | convolution fusion | flops 5436997632 | bytes 12386304 | tf_op jit(solution)/shard_map/sbf,df->sbd/dot_general | solution.py:201
  249.7 8.8 %fusion.2 = bf16[1152,2304]{1,0:T(8,128)(2,1)} fusion(bf16[512,2,2304]{2,0,1:T(8,128)(2,1)S(1)} %fusion.10, bf16[256,2,1152]{2,0,1:T(8,128)(2,1)} %collective-permute-done.4, bf16[256,2,1152]{2,0,1:T(8,128)(2,1)S(1)} %copy-done.27), kind=kOutput, calls=%fused_computation.12 | convolution fusion | flops 5443190784 | bytes 12386304 | tf_op jit(solution)/shard_map/sbd,sbf->df/dot_general | solution.py:197
  258.5 18.1 %collective-permute-done.5 = bf16[256,2,1152]{2,0,1:T(8,128)(2,1)} collective-permute-done((bf16[256,2,1152]{2,0,1:T(8,128)(2,1)}, bf16[256,2,1152]{2,0,1:T(8,128)(2,1)}, u32[]{:S(2)}, u32[]{:S(2)}) %collective-permute-start.5) | collective-permute-done | bytes 1179680 | tf_op jit(solution)/shard_map/ppermute | solution.py:89
  288.1 11.8 %fusion.31 = bf16[512,2,1152]{2,0,1:T(8,128)(2,1)} fusion(bf16[1152,2304]{1,0:T(8,128)(2,1)S(1)} %bitcast.170, f32[512,2,2304]{2,0,1:T(8,128)} %copy-done.59), kind=kOutput, calls=%fused_computation.41 | convolution fusion | flops 5458231296 | bytes 17104896 | tf_op jit(solution)/shard_map/sbf,df->sbd/dot_general | solution.py:212
  299.9 14.3 %collective-permute-done.6 = bf16[256,2,1152]{2,0,1:T(8,128)(2,1)} collective-permute-done((bf16[256,2,1152]{2,0,1:T(8,128)(2,1)}, bf16[256,2,1152]{2,0,1:T(8,128)(2,1)}, u32[]{:S(2)}, u32[]{:S(2)}) %collective-permute-start.6) | collective-permute-done | bytes 1179680 | tf_op jit(solution)/shard_map/ppermute | solution.py:69
  320.7 12.6 %multiply_reduce_fusion = (f32[2,8,512]{2,1,0:T(8,128)S(1)}, f32[2,8,512,512]{2,3,1,0:T(8,128)}) fusion(f32[2,8,512,512]{2,3,1,0:T(8,128)} %get-tuple-element.93, f32[2,8,512]{2,1,0:T(8,128)S(1)} %copy-done.30, bf16[2,512,8,72]{1,3,2,0:T(8,128)(2,1)S(1)} %bitcast.150, bf16[2,512,3,8,72]{1,4,3,2,0:T(8,128)(2,1)S(1)} %bitcast.147), kind=kOutput, calls=%fused_computation.1 | convolution fusion | flops 620748800 | bytes 35979264 | tf_op jit(solution)/shard_map/vmap(qhe,khe->hqk)/dot_general | solution.py:44
  333.2 12.5 %multiply_convert_fusion = bf16[2,8,512,512]{2,3,1,0:T(8,128)(2,1)S(1)} fusion(f32[2,8,512,512]{2,3,1,0:T(8,128)} %get-tuple-element.95, f32[2,8,512,512]{2,3,1,0:T(8,128)} %get-tuple-element.93, f32[2,8,512]{2,1,0:T(8,128)S(1)} %get-tuple-element.94, f32[2,8,512]{2,1,0:T(8,128)S(1)} %copy-done.30), kind=kLoop, calls=%fused_computation | loop fusion | flops 20971520 | bytes 42008576 | tf_op jit(solution)/shard_map/vmap()/convert_element_type | solution.py:48
  349.4 10.4 %fusion.77 = bf16[2,512,1,8,72]{1,4,3,0,2:T(8,128)(2,1)} fusion(bf16[2,512,8,72]{1,3,2,0:T(8,128)(2,1)} %bitcast.151, f32[2,8,512,512]{2,3,1,0:T(8,128)} %get-tuple-element.93, f32[2,8,512]{2,1,0:T(8,128)S(1)} %copy-done.30), kind=kOutput, calls=%fused_computation.110 | convolution fusion | flops 617152512 | bytes 19169280 | tf_op jit(solution)/shard_map/vmap(hqk,qhe->khe)/dot_general | solution.py:56
  383.2 17.8 %collective-permute-done.8 = bf16[256,2,1152]{2,0,1:T(8,128)(2,1)} collective-permute-done((bf16[256,2,1152]{2,0,1:T(8,128)(2,1)S(1)}, bf16[256,2,1152]{2,0,1:T(8,128)(2,1)}, u32[]{:S(2)}, u32[]{:S(2)}) %collective-permute-start.8) | collective-permute-done | bytes 1179680 | tf_op jit(solution)/shard_map/ppermute | solution.py:89
  401.0 8.6 %copy.116 = bf16[1152,2304]{1,0:T(8,128)(2,1)} copy(bf16[1152,2304]{0,1:T(8,128)(2,1)} %pad_maximum_fusion) | data formatting | bytes 10616832
  432.2 20.5 %all_gather.19 = bf16[32,6,576]{2,1,0:T(8,128)(2,1)S(1)} all-gather(bf16[2,6,576]{2,1,0:T(8,128)(2,1)S(1)} %add_convert_fusion.2), channel_id=1, replica_groups=mesh['dp'=16,'tensor'=2] {'dp'}, dimensions={0}, use_global_device_ids=true | all-gather | bytes 235008 | tf_op jit(solution)/shard_map/all_gather | solution.py:252
  475.4 13.9 %reduce-scatter.10.cloned.1.call-done = bf16[72,2304]{1,0:T(8,128)(2,1)} async-done(((bf16[1152,2304]{1,0:T(8,128)(2,1)}), bf16[72,2304]{1,0:T(8,128)(2,1)}) %reduce-scatter.10.cloned.1.call-update) | async-done | bytes 331792
  (252 shorter events, 150.5 us)
Async XLA Ops:
  7.2 64.8 %all-gather.5.cloned.1.call-start = ((), (), s32[]{:S(2)}) async-start(), calls=%async_computation.6 | async-start | bytes 4386816 | tf_op jit(solution)/shard_map/all_gather | solution.py:137
  9.5 97.1 %all-gather.7.cloned.1.call-start = ((), (), s32[]{:S(2)}) async-start(), calls=%async_computation.7 | async-start | bytes 1566720 | tf_op jit(solution)/shard_map/all_gather | solution.py:140
  10.2 157.7 %all-gather.11.cloned.1.call-start = ((), (), s32[]{:S(2)}) async-start(), calls=%async_computation.9 | async-start | bytes 5640192 | tf_op jit(solution)/shard_map/all_gather | solution.py:141
  12.1 37.2 %collective-permute-start = (bf16[256,2,1152]{2,0,1:T(8,128)(2,1)}, bf16[256,2,1152]{2,0,1:T(8,128)(2,1)S(1)}, u32[]{:S(2)}, u32[]{:S(2)}) collective-permute-start(bf16[256,2,1152]{2,0,1:T(8,128)(2,1)} %copy.83), channel_id=1, source_target_pairs={{0,1},{1,0},{2,3},{3,2},{4,5},{5,4},{6,7},{7,6},{8,9},{9,8},{10,11... | collective-permute-start | bytes 3538952 | tf_op jit(solution)/shard_map/ppermute | solution.py:75
  15.8 12.3 %all-to-all-start = ((bf16[2,16,72]{2,0,1:T(2,128)(2,1)}), bf16[2,16,72]{2,0,1:T(2,128)(2,1)S(1)}, u32[]{:S(2)}, u32[]{:S(2)}) async-start(bf16[2,16,72]{2,0,1:T(2,128)(2,1)} %copy.84), calls=%async_computation | async-start | bytes 16384 | tf_op jit(solution)/shard_map/all_to_all | solution.py:128
  21.7 199.2 %all-gather.9.cloned.1.call-start = ((), (), s32[]{:S(2)}) async-start(), calls=%async_computation.8 | async-start | bytes 5640192 | tf_op jit(solution)/shard_map/all_gather | solution.py:142
  22.9 81.4 %collective-permute-start.2 = (bf16[256,2,1152]{2,0,1:T(8,128)(2,1)}, bf16[256,2,1152]{2,0,1:T(8,128)(2,1)}, u32[]{:S(2)}, u32[]{:S(2)}) collective-permute-start(bf16[256,2,1152]{2,0,1:T(8,128)(2,1)} %copy.94), channel_id=1, source_target_pairs={{0,1},{1,0},{2,3},{3,2},{4,5},{5,4},{6,7},{7,6},{8,9},{9,8},{10,11... | collective-permute-start | bytes 3538952 | tf_op jit(solution)/shard_map/ppermute | solution.py:75
  30.3 19.0 %all-to-all-start.1 = ((f32[16,2,3456]{2,1,0:T(2,128)}), f32[16,2,3456]{2,1,0:T(2,128)S(1)}, u32[]{:S(2)}, u32[]{:S(2)}) async-start(f32[16,2,3456]{2,1,0:T(2,128)} %copy.87), calls=%async_computation.1 | async-start | bytes 884736 | tf_op jit(solution)/shard_map/all_to_all | solution.py:133
  34.1 437.5 %reduce-scatter.8.cloned.1.call-start = ((), (), s32[]{:S(2)}) async-start(), calls=%async_computation.11 | async-start | bytes 5640192 | tf_op jit(solution)/shard_map/reduce_scatter | solution.py:119
  34.4 37.6 %copy-start.42 = (f32[256,2]{0,1:T(2,128)}, f32[256,2]{0,1:T(2,128)S(1)}, u32[]{:S(2)}) copy-start(f32[256,2]{0,1:T(2,128)S(1)} %broadcast_multiply_fusion.6) | copy-start | bytes 6148
  34.9 37.1 %copy-start.48 = (f32[256,2]{0,1:T(2,128)}, f32[256,2]{0,1:T(2,128)S(1)}, u32[]{:S(2)}) copy-start(f32[256,2]{0,1:T(2,128)S(1)} %add_rsqrt_fusion.2) | copy-start | bytes 6148
  50.2 17.2 %collective-permute-start.1 = (f32[2,6,576]{2,1,0:T(8,128)S(1)}, f32[2,6,576]{2,1,0:T(8,128)S(1)}, u32[]{:S(2)}, u32[]{:S(2)}) collective-permute-start(f32[2,6,576]{2,1,0:T(8,128)S(1)} %reshape.132), channel_id=1, source_target_pairs={{0,1},{1,0},{2,3},{3,2},{4,5},{5,4},{6,7},{7,6},{8,9},{9,8},{10,11... | collective-permute-start | bytes 82952 | tf_op jit(solution)/shard_map/ppermute | solution.py:98
  110.3 28.2 %collective-permute-start.3 = (bf16[256,2,1152]{2,0,1:T(8,128)(2,1)S(1)}, bf16[256,2,1152]{2,0,1:T(8,128)(2,1)S(1)}, u32[]{:S(2)}, u32[]{:S(2)}) collective-permute-start(bf16[256,2,1152]{2,0,1:T(8,128)(2,1)S(1)} %slice.91), channel_id=1, source_target_pairs={{0,1},{1,0},{2,3},{3,2},{4,5},{5,4},{6,7},{7,6},{8,9},{9,8},{10,11... | collective-permute-start | bytes 3538952 | tf_op jit(solution)/shard_map/ppermute | solution.py:89
  140.5 27.5 %collective-permute-start.4 = (bf16[256,2,1152]{2,0,1:T(8,128)(2,1)S(1)}, bf16[256,2,1152]{2,0,1:T(8,128)(2,1)}, u32[]{:S(2)}, u32[]{:S(2)}) collective-permute-start(bf16[256,2,1152]{2,0,1:T(8,128)(2,1)S(1)} %add_convert_fusion.1), channel_id=1, source_target_pairs={{0,1},{1,0},{2,3},{3,2},{4,5},{5,4},{6,7},{7,6},{8,9},{9,8},{10,11... | collective-permute-start | bytes 3538952 | tf_op jit(solution)/shard_map/ppermute | solution.py:69
  221.0 252.5 %reduce-scatter.6.cloned.1.call-start = ((), (), s32[]{:S(2)}) async-start(), calls=%async_computation.10 | async-start | bytes 5640192 | tf_op jit(solution)/shard_map/reduce_scatter | solution.py:119
  248.2 28.5 %collective-permute-start.5 = (bf16[256,2,1152]{2,0,1:T(8,128)(2,1)}, bf16[256,2,1152]{2,0,1:T(8,128)(2,1)}, u32[]{:S(2)}, u32[]{:S(2)}) collective-permute-start(bf16[256,2,1152]{2,0,1:T(8,128)(2,1)} %slice.96), channel_id=1, source_target_pairs={{0,1},{1,0},{2,3},{3,2},{4,5},{5,4},{6,7},{7,6},{8,9},{9,8},{10,11... | collective-permute-start | bytes 3538952 | tf_op jit(solution)/shard_map/ppermute | solution.py:89
  286.6 27.6 %collective-permute-start.6 = (bf16[256,2,1152]{2,0,1:T(8,128)(2,1)}, bf16[256,2,1152]{2,0,1:T(8,128)(2,1)}, u32[]{:S(2)}, u32[]{:S(2)}) collective-permute-start(bf16[256,2,1152]{2,0,1:T(8,128)(2,1)} %multiply_convert_fusion.4), channel_id=1, source_target_pairs={{0,1},{1,0},{2,3},{3,2},{4,5},{5,4},{6,7},{7,6},{8,9},{9,8},{10,11... | collective-permute-start | bytes 3538952 | tf_op jit(solution)/shard_map/ppermute | solution.py:69
  299.9 189.4 %reduce-scatter.10.cloned.1.call-start = ((), (), s32[]{:S(2)}) async-start(), calls=%async_computation.12 | async-start | bytes 5640192
  317.5 47.7 %collective-permute-start.7 = (bf16[256,2,1152]{2,0,1:T(8,128)(2,1)}, bf16[256,2,1152]{2,0,1:T(8,128)(2,1)}, u32[]{:S(2)}, u32[]{:S(2)}) collective-permute-start(bf16[256,2,1152]{2,0,1:T(8,128)(2,1)} %slice.77), channel_id=1, source_target_pairs={{0,1},{1,0},{2,3},{3,2},{4,5},{5,4},{6,7},{7,6},{8,9},{9,8},{10,11... | collective-permute-start | bytes 3538952 | tf_op jit(solution)/shard_map/ppermute | solution.py:89
  374.6 26.4 %collective-permute-start.8 = (bf16[256,2,1152]{2,0,1:T(8,128)(2,1)S(1)}, bf16[256,2,1152]{2,0,1:T(8,128)(2,1)}, u32[]{:S(2)}, u32[]{:S(2)}) collective-permute-start(bf16[256,2,1152]{2,0,1:T(8,128)(2,1)S(1)} %slice.98), channel_id=1, source_target_pairs={{0,1},{1,0},{2,3},{3,2},{4,5},{5,4},{6,7},{7,6},{8,9},{9,8},{10,11... | collective-permute-start | bytes 3538952 | tf_op jit(solution)/shard_map/ppermute | solution.py:89
  420.3 39.5 %copy-start.3 = (f32[256,2,1152]{2,0,1:T(8,128)S(1)}, f32[256,2,1152]{2,0,1:T(8,128)}, u32[]{:S(2)}) copy-start(f32[256,2,1152]{2,0,1:T(8,128)} %copy-done.2) | copy-start | bytes 7077892
  427.3 4.1 collective-permute-start.9
  455.5 11.0 %all-to-all-start.2 = ((f32[16,2,72]{2,1,0:T(2,128)}), f32[16,2,72]{2,1,0:T(2,128)}, u32[]{:S(2)}, u32[]{:S(2)}) async-start(f32[16,2,72]{2,1,0:T(2,128)} %bitcast.165), calls=%async_computation.2 | async-start | bytes 32768 | tf_op jit(solution)/shard_map/all_to_all | solution.py:259
  467.3 3.7 collective-permute-start.10
  (59 other events, 419.9 us)
Sparse Core Ops, SparseCore 0:
  10.9 55.0 all-gather.4
  68.2 38.3 all-gather.6
  108.7 55.1 all-gather.10
  166.0 54.9 all-gather.8
  224.8 78.0 reduce-scatter.7
  306.8 78.5 reduce-scatter.5
  409.7 79.4 reduce-scatter.9
